TPU v7x, 256 devices: a whole 4x4x8 slice. The times are simulated.
256 devices in a mesh: refresh: 8 (over z), lists: 32 (over y, x, core).
Axes of the slice: x: 4, y: 4, z: 8, core: 2. Of those that a mesh axis runs over, the one named last changes fastest.
Arguments:
- features: bfloat16 [131072, 1024], P(('refresh', 'lists')), may hold values from -6 to 6
- w_hidden: bfloat16 [1024, 1024], P('refresh'), may hold values from -0.1875 to 0.1875
- w_out: bfloat16 [1024, 256], P('refresh'), may hold values from -0.1875 to 0.1875
- list_ids: int32 [131072], P(('refresh', 'lists')), may hold values from 0 to 4095, as said below
- centroids: bfloat16 [4096, 256], P('lists'), may hold values from -6 to 6
- queries: bfloat16 [16384, 256], P('lists'), may hold values from -0.5 to 0.5
Outputs:
- stored_codes: bfloat16 [262144, 256], P(('refresh', 'lists'))
- best: float32 [256, 16384], P(('refresh', 'lists'))
Inputs may be any that keep to these rules, and one draw needn't show every extreme that they name: `list_ids`: among the 512 items of one device, the items whose list lies in owner j's range (128 * j to 128 * j + 127) number at most 32 for every owner j, and exactly 32 for one owner.
All inputs are finite; a program needn't handle non-finite values.
Results may differ from a plain program's by a relative error of at most 0.007.
Values may be sent and summed in bfloat16 or wider, within the bound.
A program may use at most 64 MiB of HBM per device.

v0:
```python
import jax
import jax.numpy as jnp
from jax import lax
from jax.sharding import PartitionSpec as P


def root_scale(values):
    return values * lax.rsqrt(jnp.mean(values * values, axis=-1, keepdims=True) + 1e-06)


def add_rows(left, piece):
    return jnp.dot(left, piece, preferred_element_type=jnp.float32)


def best_for(query_block, block_codes, block_lists):
    direct = jnp.dot(query_block, block_codes.T, preferred_element_type=jnp.float32)
    filled = block_lists >= 0
    return jnp.max(jnp.where(filled[None, :], direct, -1e30), axis=1)


def per_device(features, w_hidden, w_out, list_ids, centroids, queries):
    count_items = features.shape[0]
    width_out = w_out.shape[1]
    inputs = features.astype(jnp.float32)
    normed = root_scale(inputs).astype(jnp.bfloat16)
    pre = add_rows(normed, lax.all_gather(w_hidden, "refresh", axis=0, tiled=True))
    hidden = (inputs + jax.nn.gelu(pre, approximate=False)).astype(jnp.bfloat16)
    hnorm = root_scale(hidden.astype(jnp.float32)).astype(jnp.bfloat16)
    projected = add_rows(hnorm, lax.all_gather(w_out, "refresh", axis=0, tiled=True))
    vectors = projected.astype(jnp.bfloat16)
    owners_count = lax.axis_size("lists")
    capacity = 2 * count_items // owners_count
    lists_dev = centroids.shape[0]
    owner = list_ids // lists_dev
    within = list_ids - owner * lists_dev
    owner_table = (owner[:, None] == jnp.arange(owners_count, dtype=jnp.int32)[None, :]).astype(
        jnp.bfloat16
    )
    positions = jnp.arange(count_items, dtype=jnp.int32)
    earlier = (positions[:, None] > positions[None, :]).astype(jnp.bfloat16)
    prior = jnp.dot(earlier, owner_table, preferred_element_type=jnp.float32)
    ranking = jnp.sum(prior * owner_table.astype(jnp.float32), axis=1).astype(jnp.int32)
    slots = owner * capacity + ranking
    send_rows = jnp.zeros((owners_count * capacity, width_out), jnp.bfloat16).at[slots].set(vectors)
    send_lists = jnp.full((owners_count * capacity,), -1, jnp.int32).at[slots].set(within)
    send_rows = send_rows.reshape(owners_count, capacity, width_out)
    send_lists = send_lists.reshape(owners_count, capacity)
    got_rows, got_lists = (
        lax.all_to_all(send_rows, "lists", split_axis=0, concat_axis=0, tiled=True),
        lax.all_to_all(send_lists, "lists", split_axis=0, concat_axis=0, tiled=True),
    )
    got_rows = got_rows.reshape(owners_count * capacity, width_out)
    got_lists = got_lists.reshape(owners_count * capacity)
    filled = got_lists >= 0
    list_table = (
        jnp.maximum(got_lists, 0)[:, None] == jnp.arange(lists_dev, dtype=jnp.int32)[None, :]
    ).astype(jnp.bfloat16)
    centre_rows = jnp.dot(list_table, centroids, preferred_element_type=jnp.float32)
    stored_codes = jnp.where(
        filled[:, None], got_rows.astype(jnp.float32) - centre_rows, 0.0
    ).astype(jnp.bfloat16)
    best = best_for(
        lax.all_gather(queries, "lists", axis=0, tiled=True), stored_codes, got_lists
    ).reshape(1, -1)
    return (stored_codes, best)


def solution(mesh):
    in_specs = (
        P(("refresh", "lists"), None),
        P("refresh", None),
        P("refresh", None),
        P(("refresh", "lists")),
        P("lists", None),
        P("lists", None),
    )
    out_specs = (P(("refresh", "lists"), None), P(("refresh", "lists"), None))
    return jax.shard_map(
        per_device, mesh=mesh, in_specs=in_specs, out_specs=out_specs, check_vma=False
    )
```

profile of v0, /device:TPU:1, one launch (start us, length us, event | category | flops | bytes accessed | tf_op | source)
XLA Modules:
  0.0 139.4 jit_solution(5882314491150482812)
XLA Ops:
  7.2 0.0 all-gather.3.cloned.1.call-start
  7.2 0.7 all-gather.3.cloned.1.call-update
  7.9 0.0 all-gather.5.cloned.1.call-start
  8.0 0.7 all-gather.5.cloned.1.call-update
  8.7 0.7 multiply_subtract_fusion
  9.4 0.3 fusion.16
  9.7 2.4 %scatter_custom_fusion = s32[1024]{0:T(1024)S(1)} fusion(s32[512]{0:T(512)S(1)} %compare_select_fusion, s32[512]{0:T(512)S(1)} %get-tuple-element.2, s32[]{:T(128)} %constant.43.clone.1), kind=kCustom, calls=%fused_computation.60 | custom fusion | bytes 4100 | tf_op jit(solution)/shard_map/scatter | solution.py:45
  12.1 0.7 all_to_all.9
  12.8 8.6 %all-to-all-start = ((s32[32,1,32]{2,1,0:T(1,128)}), s32[32,1,32]{2,1,0:T(1,128)S(1)}, u32[]{:S(2)}, u32[]{:S(2)}) async-start(s32[32,1,32]{2,1,0:T(1,128)} %all_to_all.9), calls=%async_computation | async-start | bytes 32768 | tf_op jit(solution)/shard_map/all_to_all | solution.py:50
  21.4 1.5 %fusion.2 = f32[512]{0:T(512)S(1)} fusion(bf16[512,1024]{1,0:T(8,128)(2,1)} %param.6), kind=kLoop, calls=%fused_computation.11 | loop fusion | flops 1572352 | bytes 1050624 | tf_op jit(solution)/shard_map/reduce_sum | solution.py:8
  22.9 26.6 %all_gather.10 = bf16[1024,256]{1,0:T(8,128)(2,1)S(1)} all-gather(bf16[128,256]{1,0:T(8,128)(2,1)} %param.8), channel_id=1, replica_groups=mesh['refresh'=8,'lists'=32] {'refresh'}, dimensions={0}, use_global_device_ids=true | all-gather | bytes 589824 | tf_op jit(solution)/shard_map/all_gather | solution.py:29
  49.5 4.7 %all-gather.3.cloned.1.call-done = bf16[1024,1024]{1,0:T(8,128)(2,1)} async-done(((bf16[128,1024]{1,0:T(8,128)(2,1)}), bf16[1024,1024]{1,0:T(8,128)(2,1)}) %all-gather.3.cloned.1.call-update) | async-done | bytes 2097168 | tf_op jit(solution)/shard_map/all_gather | solution.py:26
  54.2 7.6 %fusion = (f32[512]{0:T(512)S(1)}, bf16[512,1024]{1,0:T(8,128)(2,1)S(1)}) fusion(bf16[1024,1024]{1,0:T(8,128)(2,1)} %all-gather.3.cloned.1.call-done, bf16[512,1024]{1,0:T(8,128)(2,1)S(1)} %copy-done.1, f32[512]{0:T(512)S(1)} %add_rsqrt_fusion.1), kind=kOutput, calls=%fused_computation.9 | convolution fusion | flops 1112014336 | bytes 4198400 | tf_op jit(solution)/shard_map/dot_general | solution.py:12
  61.8 0.5 convolution_convert_fusion
  62.3 3.1 %scatter_custom_fusion.1 = bf16[1024,256]{1,0:T(8,128)(2,1)} fusion(s32[512]{0:T(512)S(1)} %compare_select_fusion, bf16[512,256]{1,0:T(8,128)(2,1)S(1)} %convolution_convert_fusion, bf16[]{:T(256)} %constant.17.clone.1), kind=kCustom, calls=%fused_computation.43 | custom fusion | bytes 524290 | tf_op jit(solution)/shard_map/scatter | solution.py:44
  65.5 9.7 %all-to-all-start.1 = ((bf16[32,32,256]{2,1,0:T(8,128)(2,1)}), bf16[32,32,256]{2,1,0:T(8,128)(2,1)S(1)}, u32[]{:S(2)}, u32[]{:S(2)}) async-start(bf16[32,32,256]{2,1,0:T(8,128)(2,1)} %bitcast), calls=%async_computation.1 | async-start | bytes 1048576 | tf_op jit(solution)/shard_map/all_to_all | solution.py:49
  75.1 0.1 compare_reduce_fusion
  75.2 0.1 ge.16
  75.3 0.1 maximum_reduce_fusion
  75.3 0.1 max.11
  75.4 12.4 %all-to-all-done.1 = bf16[32,32,256]{2,1,0:T(8,128)(2,1)S(1)} async-done(((bf16[32,32,256]{2,1,0:T(8,128)(2,1)}), bf16[32,32,256]{2,1,0:T(8,128)(2,1)S(1)}, u32[]{:S(2)}, u32[]{:S(2)}) %all-to-all-start.1) | async-done | bytes 524320 | tf_op jit(solution)/shard_map/all_to_all | solution.py:49
  87.8 0.4 fusion.15
  88.2 30.8 %all-gather.5.cloned.1.call-done = bf16[16384,256]{1,0:T(8,128)(2,1)} async-done(((bf16[512,256]{1,0:T(8,128)(2,1)}), bf16[16384,256]{1,0:T(8,128)(2,1)}) %all-gather.5.cloned.1.call-update) | async-done | bytes 8388624 | tf_op jit(solution)/shard_map/all_gather | solution.py:63
  119.0 13.5 %select_reduce_fusion = f32[16384]{0:T(1024)} fusion(bf16[1024,256]{1,0:T(8,128)(2,1)S(1)} %fusion.15, bf16[16384,256]{1,0:T(8,128)(2,1)} %all-gather.5.cloned.1.call-done, pred[1024]{0:T(1024)(128)(4,1)S(1)} %ge.16), kind=kOutput, calls=%fused_computation.2 | convolution fusion | flops 8623472640 | bytes 8979456 | tf_op jit(solution)/shard_map/dot_general | solution.py:16
  (10 shorter events, 0.0 us)
Async XLA Ops:
  7.2 80.6 %copy-start = (bf16[128,256]{1,0:T(8,128)(2,1)S(1)}, bf16[128,256]{1,0:T(8,128)(2,1)}, u32[]{:S(2)}) copy-start(bf16[128,256]{1,0:T(8,128)(2,1)} %param.10) | copy-start | bytes 196612
  7.2 47.0 %copy-start.1 = (bf16[512,1024]{1,0:T(8,128)(2,1)S(1)}, bf16[512,1024]{1,0:T(8,128)(2,1)}, u32[]{:S(2)}) copy-start(bf16[512,1024]{1,0:T(8,128)(2,1)} %param.6) | copy-start | bytes 3145732
  7.2 47.0 %all-gather.3.cloned.1.call-start = ((), (), s32[]{:S(2)}) async-start(), calls=%async_computation.2 | async-start | bytes 2359296 | tf_op jit(solution)/shard_map/all_gather | solution.py:26
  7.9 111.1 %all-gather.5.cloned.1.call-start = ((), (), s32[]{:S(2)}) async-start(), calls=%async_computation.3 | async-start | bytes 8650752 | tf_op jit(solution)/shard_map/all_gather | solution.py:63
  12.8 52.6 %all-to-all-start = ((s32[32,1,32]{2,1,0:T(1,128)}), s32[32,1,32]{2,1,0:T(1,128)S(1)}, u32[]{:S(2)}, u32[]{:S(2)}) async-start(s32[32,1,32]{2,1,0:T(1,128)} %all_to_all.9), calls=%async_computation | async-start | bytes 32768 | tf_op jit(solution)/shard_map/all_to_all | solution.py:50
  65.5 22.3 %all-to-all-start.1 = ((bf16[32,32,256]{2,1,0:T(8,128)(2,1)}), bf16[32,32,256]{2,1,0:T(8,128)(2,1)S(1)}, u32[]{:S(2)}, u32[]{:S(2)}) async-start(bf16[32,32,256]{2,1,0:T(8,128)(2,1)} %bitcast), calls=%async_computation.1 | async-start | bytes 1048576 | tf_op jit(solution)/shard_map/all_to_all | solution.py:49
  88.2 44.3 %copy-start.2 = (bf16[1024,256]{1,0:T(8,128)(2,1)}, bf16[1024,256]{1,0:T(8,128)(2,1)S(1)}, u32[]{:S(2)}) copy-start(bf16[1024,256]{1,0:T(8,128)(2,1)S(1)} %fusion.15) | copy-start | bytes 1572868
Sparse Core Ops, SparseCore 0:
  9.8 44.3 all-gather.2
  56.7 62.2 all-gather.4
where the time goes:
time: 140 us; the launch traced here: 139 us
  waiting for transfers between devices  49.2 us (35%)
  blocking collectives  26.6 us (19%)
  matrix products  22.2 us (16%)
  starting transfers between devices  18.3 us (13%)
  between operations  14.1 us (10%)
  local copies, waits for them, and re-layouts  6.46 us (5%)
  other arithmetic  2.33 us (2%)
    all_gather x1, waiting for transfers between devices, per_device(): lax.all_gather(queries, 'lists', axis=0, tiled=True)  30.8 us
    all_gather x1, blocking collectives, per_device(): lax.all_gather(w_out, 'refresh', axis=0, tiled=True)  26.6 us
    dot_general x1, matrix products, best_for(): jnp.dot(query_block, block_codes.T, preferred_element_type=jnp.float32)  13.5 us
    all_to_all x1, waiting for transfers between devices, per_device(): lax.all_to_all(send_rows, 'lists', split_axis=0, concat_axis=0, tiled=True)  12.4 us
    all_to_all x1, starting transfers between devices, per_device(): lax.all_to_all(send_rows, 'lists', split_axis=0, concat_axis=0, tiled=True)  9.66 us
    all_to_all x1, starting transfers between devices, per_device(): lax.all_to_all(send_lists, 'lists', split_axis=0, concat_axis=0, tiled=True)  8.59 us
    dot_general x2, matrix products, add_rows(): return jnp.dot(left, piece, preferred_element_type=jnp.float32)  8.09 us
    all_gather x1, waiting for transfers between devices, per_device(): lax.all_gather(w_hidden, 'refresh', axis=0, tiled=True)  4.65 us
  transfers between devices with their start and end apart: 4, of which 3 were waited for; matrix products, arithmetic and copies ran while one was open for 12% of the time, Pallas kernels for 0%

commit v1 on v0

v1 whole, which is shorter than its diff:
```python
import jax
import jax.numpy as jnp
from jax import lax
from jax.experimental import pallas as pl
from jax.experimental.pallas import tpu as pltpu
from jax.sharding import PartitionSpec as P

MESH = pl.DeviceIdType.MESH
NY, NX, NC, NZ = 4, 4, 2, 8
PLANE = NY * NX * NC
ITEMS, FEAT, WIDTH, LISTS, CAP = 512, 1024, 256, 128, 32
SLOTS = PLANE * CAP
WCOLS = FEAT + WIDTH
HALF = WCOLS // 2
ROWS = FEAT // NZ
F32, BF16 = jnp.float32, jnp.bfloat16


def erf(v):
    v = jnp.clip(v, -3.832506856900711, 3.832506856900711)
    s = v * v
    top = jnp.float32(0.00022905065861350646)
    for coef in (
        0.0034082910107109506,
        0.050955695062380861,
        0.18520832239976145,
        1.128379143519084,
    ):
        top = top * s + jnp.float32(coef)
    low = jnp.float32(-1.1791602954361697e-7)
    for coef in (
        0.000023547966471313185,
        0.0010179625278914885,
        0.014070470171167667,
        0.11098505178285362,
        0.49746925110067538,
        1.0,
    ):
        low = low * s + jnp.float32(coef)
    return v * top / low


def kernel(
    feat_in, wh_in, wo_in, lists_ref, cent_ref, q_in,
    codes_ref, best_ref,
    feat, wfull, normed, hid, squares, sel, send, recv, slists, glists, onehot, centre, scored, qbuf,
    loc, ws, wz_r, wp_r, wc_r, qs, q1_r, q2_r, qc_r, ls, lr, av, ar,
):
    me = lax.axis_index("lists")
    z = lax.axis_index("refresh")
    y, x, c = me // (NX * NC), (me // NC) % NX, me % NC

    def at(dy, dx, dc):
        return ((y + dy) % NY * NX + (x + dx) % NX) * NC + (c + dc) % NC

    def to(lists, refresh=None):
        return (z if refresh is None else refresh, lists)

    def push(src, dst, send_sem, recv_sem, device):
        pltpu.make_async_remote_copy(
            src_ref=src, dst_ref=dst, send_sem=send_sem, recv_sem=recv_sem,
            device_id=device, device_id_type=MESH,
        ).start()

    def await_bytes(ref, sem):
        pltpu.make_async_copy(ref, ref, sem).wait()

    barrier = pltpu.get_barrier_semaphore()

    def greet_plane(k, _):
        pl.semaphore_signal(
            barrier, inc=1, device_id=to(at(k // 8, (k // 2) % 4, k % 2)), device_id_type=MESH
        )
        return 0

    def greet_z(k, _):
        pl.semaphore_signal(barrier, inc=1, device_id=to(me, (z + k) % NZ), device_id_type=MESH)
        return 0

    lax.fori_loop(1, PLANE, greet_plane, 0)
    lax.fori_loop(1, NZ, greet_z, 0)
    mine = pl.ds(pl.multiple_of(z * ROWS, ROWS), ROWS)
    own = [
        pltpu.make_async_copy(wh_in, wfull.at[mine, pl.ds(0, FEAT)], loc.at[0]),
        pltpu.make_async_copy(wo_in, wfull.at[mine, pl.ds(FEAT, WIDTH)], loc.at[1]),
        pltpu.make_async_copy(q_in, qbuf.at[me], loc.at[2]),
        pltpu.make_async_copy(feat_in, feat, loc.at[3]),
    ]
    for copy in own:
        copy.start()
    for copy in own[:3]:
        copy.wait()
    pl.semaphore_wait(barrier, PLANE - 1 + NZ - 1)

    def piece(plane, half, index):
        row = pl.multiple_of(plane * ROWS + c * (ROWS // 2) + index * 16, 16)
        return wfull.at[pl.ds(row, 16), pl.ds(half * HALF, HALF)]

    def core_part(plane, half, core):
        row = pl.multiple_of(plane * ROWS + core * (ROWS // 2), ROWS // 2)
        return wfull.at[pl.ds(row, ROWS // 2), pl.ds(half * HALF, HALF)]

    def step(i):
        near = i // 2 + 1
        return near + (i % 2) * (NZ - 2 * near)

    def send_z(i, _):
        d = step(i)
        there = to(me, (z + d) % NZ)
        for half, index in ((0, x), (1, y)):
            part = piece(z, half, index)
            push(part, part, ws.at[0], wz_r.at[d - 1, half], there)
        return 0

    lax.fori_loop(0, NZ - 1, send_z, 0)

    def rows(block, half):
        return qbuf.at[block, pl.ds(half * 256, 256)]

    for d in (1, 3, 2):
        push(rows(me, 0), rows(me, 0), qs.at[0], q1_r.at[0, d - 1], to(at(0, d, 0)))
        push(rows(me, 1), rows(me, 1), qs.at[0], q1_r.at[1, d - 1], to(at(d, 0, 0)))
    push(qbuf.at[me], qbuf.at[me], qs.at[2], qc_r.at[0], to(at(0, 0, 1)))

    ids = lists_ref[...]
    owner = lax.shift_right_logical(ids, 7)
    within = ids - owner * LISTS
    table = (lax.broadcasted_iota(jnp.int32, (PLANE, ITEMS), 0) == owner).astype(F32)
    earlier = (
        lax.broadcasted_iota(jnp.int32, (ITEMS, ITEMS), 0)
        < lax.broadcasted_iota(jnp.int32, (ITEMS, ITEMS), 1)
    ).astype(F32)
    prior = jnp.dot(table.astype(BF16), earlier.astype(BF16), preferred_element_type=F32)
    rank = jnp.sum(prior * table, axis=0, keepdims=True).astype(jnp.int32)
    rank_table = (lax.broadcasted_iota(jnp.int32, (128, ITEMS), 0) == rank).astype(F32)
    marked = table * (within + 1).astype(F32)
    slot_lists = lax.dot_general(
        marked.astype(BF16), rank_table.astype(BF16), (((1,), (1,)), ((), ())),
        preferred_element_type=F32,
    )
    slists[...] = slot_lists.reshape(PLANE, 1, 128)

    def send_lists(k, _):
        peer = at(k // 8, (k // 2) % 4, k % 2)
        push(slists.at[peer], glists.at[me], ls, lr, to(peer))
        return 0

    lax.fori_loop(1, PLANE, send_lists, 0)
    glists[me] = slists[me]

    slot = owner * CAP + rank
    for r in range(0, SLOTS, 256):
        sel[r : r + 256, :] = (
            (lax.broadcasted_iota(jnp.int32, (256, ITEMS), 0) + r == slot).astype(F32).astype(BF16)
        )

    own[3].wait()

    def norm_rows(i, _):
        r = pl.ds(pl.multiple_of(i * 64, 64), 64)
        v = feat[r, :].astype(F32)
        scale = lax.rsqrt(jnp.mean(v * v, axis=-1, keepdims=True) + 1e-06)
        normed[r, :] = (v * scale).astype(BF16)
        return 0

    lax.fori_loop(0, ITEMS // 64, norm_rows, 0)

    def spread(i, _):
        d = step(i)
        plane = (z - d + NZ) % NZ
        for half, index in ((0, x), (1, y)):
            part = piece(plane, half, index)
            await_bytes(part, wz_r.at[d - 1, half])
            for e in (1, 3, 2):
                there = to(at(0, e, 0)) if half == 0 else to(at(e, 0, 0))
                push(part, part, ws.at[1], wp_r.at[d - 1, half, e - 1], there)
        return 0

    lax.fori_loop(0, NZ - 1, spread, 0)

    def pair(i, _):
        d = step(i)
        plane = (z - d + NZ) % NZ
        for half, index in ((0, x), (1, y)):
            for e in (1, 3, 2):
                await_bytes(piece(plane, half, (index - e + 4) % 4), wp_r.at[d - 1, half, e - 1])
            part = core_part(plane, half, c)
            push(part, part, ws.at[2], wc_r.at[d - 1, half], to(at(0, 0, 1)))
        return 0

    lax.fori_loop(0, NZ - 1, pair, 0)

    for e in range(4):
        if e:
            await_bytes(rows(at(0, -e + 4, 0), 0), q1_r.at[0, e - 1])
            await_bytes(rows(at(-e + 4, 0, 0), 1), q1_r.at[1, e - 1])
        for d in (1, 3, 2):
            a, b = rows(at(0, 4 - e, 0), 0), rows(at(4 - e, 0, 0), 1)
            push(a, a, qs.at[1], q2_r.at[0, e, d - 1], to(at(d, 0, 0)))
            push(b, b, qs.at[1], q2_r.at[1, e, d - 1], to(at(0, d, 0)))

    def paired(i, _):
        d = step(i)
        plane = (z - d + NZ) % NZ
        for half in range(2):
            await_bytes(core_part(plane, half, 1 - c), wc_r.at[d - 1, half])
        return 0

    lax.fori_loop(0, NZ - 1, paired, 0)

    squares[...] = jnp.zeros_like(squares)

    def hidden(n, _):
        i, j = n % 2, n // 2
        r = pl.ds(pl.multiple_of(i * 256, 256), 256)
        cols = pl.ds(pl.multiple_of(j * 256, 256), 256)
        pre = jnp.dot(normed[r, :], wfull[:, cols], preferred_element_type=F32)
        gelu = 0.5 * pre * (1.0 + erf(pre * 0.7071067811865476))
        h = (feat[r, cols].astype(F32) + gelu).astype(BF16)
        hid[r, cols] = h
        h = h.astype(F32)
        h = h * h
        squares[r, :] += h[:, :128] + h[:, 128:]
        return 0

    lax.fori_loop(0, 8, hidden, 0)

    def vectors(i, _):
        r = pl.ds(pl.multiple_of(i * 128, 128), 128)
        total = jnp.sum(squares[r, :], axis=-1, keepdims=True)
        scale = lax.rsqrt(total * (1.0 / FEAT) + 1e-06)
        hnorm = (hid[r, :].astype(F32) * scale).astype(BF16)
        out = jnp.dot(hnorm, wfull[:, pl.ds(FEAT, WIDTH)], preferred_element_type=F32)
        normed[r, pl.ds(0, WIDTH)] = out.astype(BF16)
        return 0

    lax.fori_loop(0, 4, vectors, 0)

    def fill(i, _):
        r = pl.ds(pl.multiple_of(i * 256, 256), 256)
        out = jnp.dot(sel[r, :], normed[:, pl.ds(0, WIDTH)], preferred_element_type=F32)
        send[pl.ds(i * 8, 8)] = out.astype(BF16).reshape(8, CAP, WIDTH)
        return 0

    lax.fori_loop(0, 4, fill, 0)

    def route(k, _):
        peer = at(k // 8, (k // 2) % 4, k % 2)
        push(send.at[peer], recv.at[me], av, ar, to(peer))
        return 0

    lax.fori_loop(1, PLANE, route, 0)
    recv[me] = send[me]

    await_bytes(glists.at[pl.ds(0, PLANE - 1)], lr)
    marks = jnp.transpose(glists[...].reshape(PLANE, 128))
    lane = lax.broadcasted_iota(jnp.int32, (CAP, LISTS), 1).astype(F32) + 1.0
    for s in range(PLANE):
        column = marks[:CAP, s : s + 1]
        onehot[s * CAP : (s + 1) * CAP, :] = (column == lane).astype(F32).astype(BF16)
    centre[...] = jnp.dot(onehot[...], cent_ref[...], preferred_element_type=F32)
    filled = jnp.sum(onehot[...].astype(F32), axis=1, keepdims=True) > 0.5
    places = lax.broadcasted_iota(jnp.int32, (SLOTS, 1), 0).astype(F32)
    first = jnp.min(jnp.where(filled, places, 2.0 * SLOTS), axis=0, keepdims=True)
    some = first < SLOTS

    await_bytes(recv.at[pl.ds(0, PLANE - 1)], ar)
    codes = (recv[...].reshape(SLOTS, WIDTH).astype(F32) - centre[...]).astype(BF16)
    codes_ref[...] = codes
    codes = codes.astype(F32)
    spare = jnp.sum(jnp.where(places == first, codes, 0.0), axis=0, keepdims=True)
    scored[...] = jnp.where(filled, codes, spare).astype(BF16)

    def score(block):
        top = None
        for r in range(0, SLOTS, 256):
            s = lax.dot_general(
                scored[r : r + 256, :], qbuf[block], (((1,), (1,)), ((), ())),
                preferred_element_type=F32,
            )
            s = jnp.max(s.reshape(32, 8, 512), axis=0)
            top = s if top is None else jnp.maximum(top, s)
        top = jnp.max(top, axis=0, keepdims=True)
        best_ref[:, pl.ds(pl.multiple_of(block * 512, 512), 512)] = jnp.where(some, top, -1e30)

    score(me)
    await_bytes(qbuf.at[0], qc_r.at[0])
    score(at(0, 0, 1))

    for k in range(1, 16):
        dy, dx = k // 4, k % 4
        block = at(4 - dy, 4 - dx, 0)
        if dy > 0:
            await_bytes(rows(block, 0), q2_r.at[0, dx, dy - 1])
        if dx > 0:
            await_bytes(rows(block, 1), q2_r.at[1, dy, dx - 1])
        push(qbuf.at[block], qbuf.at[block], qs.at[2], qc_r.at[k], to(at(0, 0, 1)))

    def rest(k, _):
        dy, dx = k // 4, k % 4
        score(at(4 - dy, 4 - dx, 0))
        block = at(4 - dy, 4 - dx, 1)
        await_bytes(qbuf.at[block], qc_r.at[k])
        score(block)
        return 0

    lax.fori_loop(1, 16, rest, 0)

    await_bytes(wfull.at[pl.ds(0, 112)], ws.at[0])
    await_bytes(wfull.at[pl.ds(0, 336)], ws.at[1])
    await_bytes(wfull.at[pl.ds(0, 448)], ws.at[2])
    await_bytes(qbuf.at[pl.ds(0, 3)], qs.at[0])
    await_bytes(qbuf.at[pl.ds(0, 12)], qs.at[1])
    await_bytes(qbuf.at[pl.ds(0, 16)], qs.at[2])
    await_bytes(slists.at[pl.ds(0, PLANE - 1)], ls)
    await_bytes(send.at[pl.ds(0, PLANE - 1)], av)


def per_device(features, w_hidden, w_out, list_ids, centroids, queries):
    anywhere, vmem = pl.BlockSpec(memory_space=pl.ANY), pl.BlockSpec(memory_space=pltpu.VMEM)
    dma = pltpu.SemaphoreType.DMA
    return pl.pallas_call(
        kernel,
        out_shape=(
            jax.ShapeDtypeStruct((SLOTS, WIDTH), BF16),
            jax.ShapeDtypeStruct((1, PLANE * ITEMS), F32),
        ),
        in_specs=[anywhere, anywhere, anywhere, vmem, vmem, anywhere],
        out_specs=(vmem, vmem),
        scratch_shapes=[
            pltpu.VMEM((ITEMS, FEAT), BF16),
            pltpu.VMEM((FEAT, WCOLS), BF16),
            pltpu.VMEM((ITEMS, FEAT), BF16),
            pltpu.VMEM((ITEMS, FEAT), BF16),
            pltpu.VMEM((ITEMS, 128), F32),
            pltpu.VMEM((SLOTS, ITEMS), BF16),
            pltpu.VMEM((PLANE, CAP, WIDTH), BF16),
            pltpu.VMEM((PLANE, CAP, WIDTH), BF16),
            pltpu.VMEM((PLANE, 1, 128), F32),
            pltpu.VMEM((PLANE, 1, 128), F32),
            pltpu.VMEM((SLOTS, LISTS), BF16),
            pltpu.VMEM((SLOTS, WIDTH), F32),
            pltpu.VMEM((SLOTS, WIDTH), BF16),
            pltpu.VMEM((PLANE, ITEMS, WIDTH), BF16),
            dma((4,)), dma((3,)), dma((7, 2)), dma((7, 2, 3)), dma((7, 2)),
            dma((3,)), dma((2, 3)), dma((2, 4, 3)), dma((16,)),
            dma, dma, dma, dma,
        ],
        compiler_params=pltpu.CompilerParams(
            collective_id=0, has_side_effects=True, vmem_limit_bytes=50 * 2**20
        ),
        name="refresh",
    )(features, w_hidden, w_out, list_ids.reshape(1, ITEMS), centroids, queries)


def solution(mesh):
    in_specs = (
        P(("refresh", "lists"), None),
        P("refresh", None),
        P("refresh", None),
        P(("refresh", "lists")),
        P("lists", None),
        P("lists", None),
    )
    out_specs = (P(("refresh", "lists"), None), P(("refresh", "lists"), None))
    return jax.shard_map(
        per_device, mesh=mesh, in_specs=in_specs, out_specs=out_specs, check_vma=False
    )
```

time: 140 us -> 81.9 us (0.59)
  Pallas kernels: 0 us -> 74 us
  waiting for transfers between devices: 49.2 us -> 0 us
  blocking collectives: 26.6 us -> 0 us
  matrix products: 22.2 us -> 0 us
  starting transfers between devices: 18.3 us -> 0 us
  between operations: 14.1 us -> 0.65 us
  other arithmetic: 2.33 us -> 0 us
    pallas_call x0 -> x1, Pallas kernels: none -> 74 us  [per_device(): pl.pallas_call(kernel, out_shape=(jax.ShapeDtypeStruct((SLOTS, WIDTH), BF...]
    all_gather x2 -> x0, waiting for transfers between devices: 35.5 us -> none  [the longest x1 30.8 us: per_device(): lax.all_gather(queries, 'lists', axis=0, tiled=True)]
    all_gather x1 -> x0, blocking collectives: 26.6 us -> none  [per_device(): lax.all_gather(w_out, 'refresh', axis=0, tiled=True)]
    dot_general x5 -> x0, matrix products: 22.2 us -> none  [the longest x1 13.5 us: best_for(): jnp.dot(query_block, block_codes.T, preferred_element_type=jnp.float32)]
    all_to_all x2 -> x0, starting transfers between devices: 18.2 us -> none  [the longest x1 9.66 us: per_device(): lax.all_to_all(send_rows, 'lists', split_axis=0, concat_axis=0, tiled=True)]
    all_to_all x2 -> x0, waiting for transfers between devices: 12.4 us -> none  [the longest x1 12.4 us: per_device(): lax.all_to_all(send_rows, 'lists', split_axis=0, concat_axis=0, tiled=True)]
    unnamed x6 -> x14, local copies, waits for them, and re-layouts: 0.02 us -> 6.9 us
    scatter x2 -> x0, local copies, waits for them, and re-layouts: 5.58 us -> none  [the longest x1 3.14 us: per_device(): jnp.zeros((owners_count * capacity, width_out), jnp.bfloat16).at[slots]]
  transfers between devices with their start and end apart: 4 -> 0, of which waited for: 3 -> 0; matrix products, arithmetic and copies ran while one was open for 12% -> 0% of each run, Pallas kernels for 0% -> 0%
where the time goes in v1:
time: 81.9 us; the launch traced here: 81.6 us
  Pallas kernels  74 us (90%)
  local copies, waits for them, and re-layouts  6.9 us (8%)
    pallas_call x1, Pallas kernels, per_device(): pl.pallas_call(kernel, out_shape=(jax.ShapeDtypeStruct((SLOTS, WIDTH), BF...  74 us
    unnamed x14, local copies, waits for them, and re-layouts  6.9 us

profile of v1, /device:TPU:1, one launch (start us, length us, event | category | flops | bytes accessed | tf_op | source)
XLA Modules:
  0.0 81.6 jit_solution(7387567498721763635)
XLA Ops:
  0.6 0.0 copy-start
  0.6 1.2 %copy-done = bf16[512,1024]{1,0:T(8,128)(2,1)S(1)} copy-done((bf16[512,1024]{1,0:T(8,128)(2,1)S(1)}, bf16[512,1024]{1,0:T(8,128)(2,1)}, u32[]{:S(2)}) %copy-start) | copy-done | bytes 1048600
  1.9 0.0 copy-start.1
  1.9 0.9 %copy-done.1 = bf16[128,1024]{1,0:T(8,128)(2,1)S(1)} copy-done((bf16[128,1024]{1,0:T(8,128)(2,1)S(1)}, bf16[128,1024]{1,0:T(8,128)(2,1)}, u32[]{:S(2)}) %copy-start.1) | copy-done | bytes 262168
  2.8 0.0 copy-start.2
  2.8 0.9 %copy-done.2 = bf16[512,256]{1,0:T(8,128)(2,1)S(1)} copy-done((bf16[512,256]{1,0:T(8,128)(2,1)S(1)}, bf16[512,256]{1,0:T(8,128)(2,1)}, u32[]{:S(2)}) %copy-start.2) | copy-done | bytes 262168
  3.8 0.0 copy-start.3
  3.8 0.8 %copy-done.3 = bf16[128,256]{1,0:T(8,128)(2,1)S(1)} copy-done((bf16[128,256]{1,0:T(8,128)(2,1)S(1)}, bf16[128,256]{1,0:T(8,128)(2,1)}, u32[]{:S(2)}) %copy-start.3) | copy-done | bytes 65560
  4.6 0.0 copy-start.4
  4.6 0.8 %copy-done.4 = bf16[128,256]{1,0:T(8,128)(2,1)S(1)} copy-done((bf16[128,256]{1,0:T(8,128)(2,1)S(1)}, bf16[128,256]{1,0:T(8,128)(2,1)}, u32[]{:S(2)}) %copy-start.4) | copy-done | bytes 65560
  5.4 0.0 copy-start.5
  5.4 0.7 copy-done.5
  6.1 74.0 %refresh.1 = (bf16[1024,256]{1,0:T(8,128)(2,1)S(1)}, f32[1,16384]{1,0:T(1,128)S(1)}) custom-call(bf16[512,1024]{1,0:T(8,128)(2,1)S(1)} %copy-done, bf16[128,1024]{1,0:T(8,128)(2,1)S(1)} %copy-done.1, bf16[128,256]{1,0:T(8,128)(2,1)S(1)} %copy-done.3, s32[1,512]{1,0:T(1,128)S(1)} %bitcast.1, bf16[128,256]{1,0:T(8,128)(2,1)S(1)} %copy-done.4, ...), custom_call_target="tpu_custom_call" | custom-call | tf_op jit(solution)/shard_map/refresh/pallas_call | solution.py:322
  80.1 0.8 copy.10
  80.9 0.6 copy.11
Async XLA Ops:
  0.6 1.2 %copy-start = (bf16[512,1024]{1,0:T(8,128)(2,1)S(1)}, bf16[512,1024]{1,0:T(8,128)(2,1)}, u32[]{:S(2)}) copy-start(bf16[512,1024]{1,0:T(8,128)(2,1)} %feat_in.1) | copy-start | bytes 3145732
  1.9 0.9 %copy-start.1 = (bf16[128,1024]{1,0:T(8,128)(2,1)S(1)}, bf16[128,1024]{1,0:T(8,128)(2,1)}, u32[]{:S(2)}) copy-start(bf16[128,1024]{1,0:T(8,128)(2,1)} %wh_in.1) | copy-start | bytes 786436
  2.8 0.9 %copy-start.2 = (bf16[512,256]{1,0:T(8,128)(2,1)S(1)}, bf16[512,256]{1,0:T(8,128)(2,1)}, u32[]{:S(2)}) copy-start(bf16[512,256]{1,0:T(8,128)(2,1)} %q_in.1) | copy-start | bytes 786436
  3.8 0.8 %copy-start.3 = (bf16[128,256]{1,0:T(8,128)(2,1)S(1)}, bf16[128,256]{1,0:T(8,128)(2,1)}, u32[]{:S(2)}) copy-start(bf16[128,256]{1,0:T(8,128)(2,1)} %wo_in.1) | copy-start | bytes 196612
  4.6 0.8 %copy-start.4 = (bf16[128,256]{1,0:T(8,128)(2,1)S(1)}, bf16[128,256]{1,0:T(8,128)(2,1)}, u32[]{:S(2)}) copy-start(bf16[128,256]{1,0:T(8,128)(2,1)} %cent_ref.1) | copy-start | bytes 196612
  5.4 0.7 copy-start.5

commit v2 on v1

--- a/solution.py
+++ b/solution.py
@@ -41,9 +41,9 @@
 
 
 def kernel(
-    feat_in, wh_in, wo_in, lists_ref, cent_ref, q_in,
-    codes_ref, best_ref,
-    feat, wfull, normed, hid, squares, sel, send, recv, slists, glists, onehot, centre, scored, qbuf,
+    feat_in, wh_in, wo_in, lists_in, cent_in, q_in,
+    recv, q_out, centre_out, place_out, count_out,
+    feat, wfull, normed, hid, squares, sel, send, ids_ref, cent, slists, glists, onehot, centre, place, count,
     loc, ws, wz_r, wp_r, wc_r, qs, q1_r, q2_r, qc_r, ls, lr, av, ar,
 ):
     me = lax.axis_index("lists")
@@ -83,8 +83,10 @@
     own = [
         pltpu.make_async_copy(wh_in, wfull.at[mine, pl.ds(0, FEAT)], loc.at[0]),
         pltpu.make_async_copy(wo_in, wfull.at[mine, pl.ds(FEAT, WIDTH)], loc.at[1]),
-        pltpu.make_async_copy(q_in, qbuf.at[me], loc.at[2]),
+        pltpu.make_async_copy(lists_in, ids_ref, loc.at[2]),
         pltpu.make_async_copy(feat_in, feat, loc.at[3]),
+        pltpu.make_async_copy(cent_in, cent, loc.at[4]),
+        pltpu.make_async_copy(q_in, q_out.at[me], loc.at[5]),
     ]
     for copy in own:
         copy.start()
@@ -115,14 +117,41 @@
     lax.fori_loop(0, NZ - 1, send_z, 0)
 
     def rows(block, half):
-        return qbuf.at[block, pl.ds(half * 256, 256)]
-
-    for d in (1, 3, 2):
-        push(rows(me, 0), rows(me, 0), qs.at[0], q1_r.at[0, d - 1], to(at(0, d, 0)))
-        push(rows(me, 1), rows(me, 1), qs.at[0], q1_r.at[1, d - 1], to(at(d, 0, 0)))
-    push(qbuf.at[me], qbuf.at[me], qs.at[2], qc_r.at[0], to(at(0, 0, 1)))
-
-    ids = lists_ref[...]
+        return q_out.at[block, pl.ds(half * 256, 256)]
+
+    def own_rows(half):
+        return q_in.at[pl.ds(half * 256, 256)]
+
+    def over(half, d):
+        return to(at(0, d, 0)) if half == 0 else to(at(d, 0, 0))
+
+    def first_leg(half, d):
+        push(own_rows(half), rows(me, half), qs.at[0], q1_r.at[half, d - 1], over(half, d))
+
+    def second_leg(half, e, d):
+        block = at(0, 4 - e, 0) if half == 0 else at(4 - e, 0, 0)
+        src = rows(block, half) if e else own_rows(half)
+        push(src, rows(block, half), qs.at[1], q2_r.at[half, e, d - 1], over(1 - half, d))
+
+    def arrived(half, e, d):
+        block = at(4 - d, 4 - e, 0) if half == 0 else at(4 - e, 4 - d, 0)
+        await_bytes(rows(block, half), q2_r.at[half, e, d - 1])
+        return block
+
+    def pass_on(half, e, d):
+        block = arrived(half, e, d)
+        push(rows(block, half), rows(block, half), qs.at[1], q2_r.at[half, e, 1], over(1 - half, d))
+
+    for half in range(2):
+        for d in (1, 3):
+            first_leg(half, d)
+    for half in range(2):
+        second_leg(half, 0, 1)
+        first_leg(half, 2)
+        second_leg(half, 0, 3)
+    push(q_in, q_out.at[me], qs.at[2], qc_r.at[0], to(at(0, 0, 1)))
+
+    ids = ids_ref[...]
     owner = lax.shift_right_logical(ids, 7)
     within = ids - owner * LISTS
     table = (lax.broadcasted_iota(jnp.int32, (PLANE, ITEMS), 0) == owner).astype(F32)
@@ -178,6 +207,15 @@
 
     lax.fori_loop(0, NZ - 1, spread, 0)
 
+    for e, d in ((1, 1), (3, 3), (2, 3), (1, 3), (3, 1), (2, 1)):
+        for half in range(2):
+            if (e, d) in ((1, 1), (3, 3), (2, 3)):
+                block = at(0, 4 - e, 0) if half == 0 else at(4 - e, 0, 0)
+                await_bytes(rows(block, half), q1_r.at[half, e - 1])
+            second_leg(half, e, d)
+    for half in range(2):
+        pass_on(half, 0, 1)
+
     def pair(i, _):
         d = step(i)
         plane = (z - d + NZ) % NZ
@@ -190,14 +228,42 @@
 
     lax.fori_loop(0, NZ - 1, pair, 0)
 
-    for e in range(4):
-        if e:
-            await_bytes(rows(at(0, -e + 4, 0), 0), q1_r.at[0, e - 1])
-            await_bytes(rows(at(-e + 4, 0, 0), 1), q1_r.at[1, e - 1])
-        for d in (1, 3, 2):
-            a, b = rows(at(0, 4 - e, 0), 0), rows(at(4 - e, 0, 0), 1)
-            push(a, a, qs.at[1], q2_r.at[0, e, d - 1], to(at(d, 0, 0)))
-            push(b, b, qs.at[1], q2_r.at[1, e, d - 1], to(at(0, d, 0)))
+    own[4].wait()
+    await_bytes(glists.at[pl.ds(0, PLANE - 1)], lr)
+    marks = jnp.transpose(glists[...].reshape(PLANE, 128))
+    lane = lax.broadcasted_iota(jnp.int32, (CAP, LISTS), 1).astype(F32) + 1.0
+    for s in range(PLANE):
+        column = marks[:CAP, s : s + 1]
+        onehot[s * CAP : (s + 1) * CAP, :] = (column == lane).astype(F32).astype(BF16)
+    centre[...] = jnp.dot(onehot[...], cent[...], preferred_element_type=F32).astype(BF16)
+    held = jnp.sum((marks > 0.5).astype(F32), axis=0, keepdims=True)
+    below = (
+        lax.broadcasted_iota(jnp.int32, (PLANE, PLANE), 0)
+        < lax.broadcasted_iota(jnp.int32, (PLANE, PLANE), 1)
+    ).astype(F32)
+    start = jnp.dot(held.astype(BF16), below.astype(BF16), preferred_element_type=F32)
+    high = jnp.floor(start * (1.0 / CAP))
+    low = start - high * CAP
+    source = lax.shift_right_logical(lax.broadcasted_iota(jnp.int32, (PLANE, SLOTS), 1), 5)
+    member = (lax.broadcasted_iota(jnp.int32, (PLANE, SLOTS), 0) == source).astype(F32).astype(BF16)
+
+    def spread_out(row):
+        return jnp.dot(row.astype(BF16), member, preferred_element_type=F32)
+
+    within_source = (lax.broadcasted_iota(jnp.int32, (1, SLOTS), 1) & (CAP - 1)).astype(F32)
+    place[...] = jnp.where(
+        within_source < spread_out(held),
+        spread_out(high) * CAP + spread_out(low) + within_source,
+        -1.0,
+    )
+    count[...] = jnp.broadcast_to(jnp.sum(held, axis=1, keepdims=True), (1, 128)).astype(jnp.int32)
+    results = [
+        pltpu.make_async_copy(centre, centre_out, loc.at[6]),
+        pltpu.make_async_copy(place, place_out, loc.at[7]),
+        pltpu.make_async_copy(count, count_out, loc.at[8]),
+    ]
+    for copy in results:
+        copy.start()
 
     def paired(i, _):
         d = step(i)
@@ -225,6 +291,10 @@
 
     lax.fori_loop(0, 8, hidden, 0)
 
+    for e, d in ((1, 1), (3, 3), (2, 3)):
+        for half in range(2):
+            pass_on(half, e, d)
+
     def vectors(i, _):
         r = pl.ds(pl.multiple_of(i * 128, 128), 128)
         total = jnp.sum(squares[r, :], axis=-1, keepdims=True)
@@ -250,83 +320,89 @@
         return 0
 
     lax.fori_loop(1, PLANE, route, 0)
-    recv[me] = send[me]
-
-    await_bytes(glists.at[pl.ds(0, PLANE - 1)], lr)
-    marks = jnp.transpose(glists[...].reshape(PLANE, 128))
-    lane = lax.broadcasted_iota(jnp.int32, (CAP, LISTS), 1).astype(F32) + 1.0
-    for s in range(PLANE):
-        column = marks[:CAP, s : s + 1]
-        onehot[s * CAP : (s + 1) * CAP, :] = (column == lane).astype(F32).astype(BF16)
-    centre[...] = jnp.dot(onehot[...], cent_ref[...], preferred_element_type=F32)
-    filled = jnp.sum(onehot[...].astype(F32), axis=1, keepdims=True) > 0.5
-    places = lax.broadcasted_iota(jnp.int32, (SLOTS, 1), 0).astype(F32)
-    first = jnp.min(jnp.where(filled, places, 2.0 * SLOTS), axis=0, keepdims=True)
-    some = first < SLOTS
-
+    keep = pltpu.make_async_copy(send.at[me], recv.at[me], loc.at[9])
+    keep.start()
+
+    own[5].wait()
+    for dy, dx in sorted(
+        ((k // 4, k % 4) for k in range(1, 16)), key=lambda p: (p[0] == 2) + (p[1] == 2)
+    ):
+        block = at(4 - dy, 4 - dx, 0)
+        if dy > 0 and not (dx in (0, 1) and dy == 1 or dx in (2, 3) and dy == 3):
+            arrived(0, dx, dy)
+        if dx > 0 and not (dy in (0, 1) and dx == 1 or dy in (2, 3) and dx == 3):
+            arrived(1, dy, dx)
+        push(q_out.at[block], q_out.at[block], qs.at[2], qc_r.at[dy * 4 + dx], to(at(0, 0, 1)))
+    for k in range(16):
+        await_bytes(q_out.at[at(4 - k // 4, 4 - k % 4, 1)], qc_r.at[k])
     await_bytes(recv.at[pl.ds(0, PLANE - 1)], ar)
-    codes = (recv[...].reshape(SLOTS, WIDTH).astype(F32) - centre[...]).astype(BF16)
-    codes_ref[...] = codes
-    codes = codes.astype(F32)
-    spare = jnp.sum(jnp.where(places == first, codes, 0.0), axis=0, keepdims=True)
-    scored[...] = jnp.where(filled, codes, spare).astype(BF16)
-
-    def score(block):
-        top = None
-        for r in range(0, SLOTS, 256):
-            s = lax.dot_general(
-                scored[r : r + 256, :], qbuf[block], (((1,), (1,)), ((), ())),
-                preferred_element_type=F32,
-            )
-            s = jnp.max(s.reshape(32, 8, 512), axis=0)
-            top = s if top is None else jnp.maximum(top, s)
-        top = jnp.max(top, axis=0, keepdims=True)
-        best_ref[:, pl.ds(pl.multiple_of(block * 512, 512), 512)] = jnp.where(some, top, -1e30)
-
-    score(me)
-    await_bytes(qbuf.at[0], qc_r.at[0])
-    score(at(0, 0, 1))
-
-    for k in range(1, 16):
-        dy, dx = k // 4, k % 4
-        block = at(4 - dy, 4 - dx, 0)
-        if dy > 0:
-            await_bytes(rows(block, 0), q2_r.at[0, dx, dy - 1])
-        if dx > 0:
-            await_bytes(rows(block, 1), q2_r.at[1, dy, dx - 1])
-        push(qbuf.at[block], qbuf.at[block], qs.at[2], qc_r.at[k], to(at(0, 0, 1)))
-
-    def rest(k, _):
-        dy, dx = k // 4, k % 4
-        score(at(4 - dy, 4 - dx, 0))
-        block = at(4 - dy, 4 - dx, 1)
-        await_bytes(qbuf.at[block], qc_r.at[k])
-        score(block)
-        return 0
-
-    lax.fori_loop(1, 16, rest, 0)
 
     await_bytes(wfull.at[pl.ds(0, 112)], ws.at[0])
     await_bytes(wfull.at[pl.ds(0, 336)], ws.at[1])
     await_bytes(wfull.at[pl.ds(0, 448)], ws.at[2])
-    await_bytes(qbuf.at[pl.ds(0, 3)], qs.at[0])
-    await_bytes(qbuf.at[pl.ds(0, 12)], qs.at[1])
-    await_bytes(qbuf.at[pl.ds(0, 16)], qs.at[2])
+    await_bytes(q_out.at[pl.ds(0, 3)], qs.at[0])
+    await_bytes(q_out.at[pl.ds(0, 12)], qs.at[1])
+    await_bytes(q_out.at[pl.ds(0, 16)], qs.at[2])
     await_bytes(slists.at[pl.ds(0, PLANE - 1)], ls)
     await_bytes(send.at[pl.ds(0, PLANE - 1)], av)
+    keep.wait()
+    for copy in results:
+        copy.wait()
+
+
+VARIANTS = (256, 512, 576, 640, 704, 768, 1024)
+TILE = 4096
+
+
+def score_kernel(count_ref, recv_ref, centre_ref, place_ref, q_ref, codes_ref, best_ref, packed):
+    count = count_ref[0, 0]
+
+    @pl.when(pl.program_id(0) == 0)
+    def _():
+        codes = (recv_ref[...].astype(F32) - centre_ref[...].astype(F32)).astype(BF16)
+        codes_ref[...] = codes
+        last = jnp.maximum(count - 1, 0)
+        for r in range(0, SLOTS, 128):
+
+            @pl.when((r == 0) | (r < count + 127))
+            def _():
+                row = jnp.minimum(lax.broadcasted_iota(jnp.int32, (128, SLOTS), 0) + r, last)
+                pick = (row.astype(F32) == place_ref[...]).astype(F32).astype(BF16)
+                packed[r : r + 128, :] = jnp.dot(
+                    pick, codes, preferred_element_type=F32
+                ).astype(BF16)
+
+    for at, size in enumerate(VARIANTS):
+        less = VARIANTS[at - 1] if at else -1
+
+        @pl.when((count > less) & (count <= size))
+        def _():
+            for lo in range(0, TILE, 256):
+                s = lax.dot_general(
+                    packed[:size, :], q_ref[lo : lo + 256, :], (((1,), (1,)), ((), ())),
+                    preferred_element_type=F32,
+                )
+                best_ref[:, lo : lo + 256] = jnp.max(s, axis=0, keepdims=True)
+
+    @pl.when(count == 0)
+    def _():
+        best_ref[...] = jnp.full_like(best_ref, -1e30)
 
 
 def per_device(features, w_hidden, w_out, list_ids, centroids, queries):
-    anywhere, vmem = pl.BlockSpec(memory_space=pl.ANY), pl.BlockSpec(memory_space=pltpu.VMEM)
+    anywhere = pl.BlockSpec(memory_space=pl.ANY)
     dma = pltpu.SemaphoreType.DMA
-    return pl.pallas_call(
+    recv, q_all, centre, place, count = pl.pallas_call(
         kernel,
         out_shape=(
+            jax.ShapeDtypeStruct((PLANE, CAP, WIDTH), BF16),
+            jax.ShapeDtypeStruct((PLANE, ITEMS, WIDTH), BF16),
             jax.ShapeDtypeStruct((SLOTS, WIDTH), BF16),
-            jax.ShapeDtypeStruct((1, PLANE * ITEMS), F32),
+            jax.ShapeDtypeStruct((1, SLOTS), F32),
+            jax.ShapeDtypeStruct((1, 128), jnp.int32),
         ),
-        in_specs=[anywhere, anywhere, anywhere, vmem, vmem, anywhere],
-        out_specs=(vmem, vmem),
+        in_specs=[anywhere] * 6,
+        out_specs=(anywhere,) * 5,
         scratch_shapes=[
             pltpu.VMEM((ITEMS, FEAT), BF16),
             pltpu.VMEM((FEAT, WCOLS), BF16),
@@ -335,22 +411,49 @@
             pltpu.VMEM((ITEMS, 128), F32),
             pltpu.VMEM((SLOTS, ITEMS), BF16),
             pltpu.VMEM((PLANE, CAP, WIDTH), BF16),
-            pltpu.VMEM((PLANE, CAP, WIDTH), BF16),
+            pltpu.VMEM((1, ITEMS), jnp.int32),
+            pltpu.VMEM((LISTS, WIDTH), BF16),
             pltpu.VMEM((PLANE, 1, 128), F32),
             pltpu.VMEM((PLANE, 1, 128), F32),
             pltpu.VMEM((SLOTS, LISTS), BF16),
-            pltpu.VMEM((SLOTS, WIDTH), F32),
             pltpu.VMEM((SLOTS, WIDTH), BF16),
-            pltpu.VMEM((PLANE, ITEMS, WIDTH), BF16),
-            dma((4,)), dma((3,)), dma((7, 2)), dma((7, 2, 3)), dma((7, 2)),
+            pltpu.VMEM((1, SLOTS), F32),
+            pltpu.VMEM((1, 128), jnp.int32),
+            dma((10,)), dma((3,)), dma((7, 2)), dma((7, 2, 3)), dma((7, 2)),
             dma((3,)), dma((2, 3)), dma((2, 4, 3)), dma((16,)),
             dma, dma, dma, dma,
         ],
         compiler_params=pltpu.CompilerParams(
-            collective_id=0, has_side_effects=True, vmem_limit_bytes=50 * 2**20
+            collective_id=0, has_side_effects=True, vmem_limit_bytes=62 * 2**20
         ),
-        name="refresh",
+        name="encode_and_route",
     )(features, w_hidden, w_out, list_ids.reshape(1, ITEMS), centroids, queries)
+    whole = lambda *shape: pl.BlockSpec(shape, lambda i: (0,) * len(shape))
+    return pl.pallas_call(
+        score_kernel,
+        grid=(PLANE * ITEMS // TILE,),
+        out_shape=(
+            jax.ShapeDtypeStruct((SLOTS, WIDTH), BF16),
+            jax.ShapeDtypeStruct((1, PLANE * ITEMS), F32),
+        ),
+        in_specs=[
+            pl.BlockSpec(memory_space=pltpu.SMEM),
+            whole(SLOTS, WIDTH),
+            whole(SLOTS, WIDTH),
+            whole(1, SLOTS),
+            pl.BlockSpec((TILE, WIDTH), lambda i: (i, 0)),
+        ],
+        out_specs=(whole(SLOTS, WIDTH), pl.BlockSpec((1, TILE), lambda i: (0, i))),
+        scratch_shapes=[pltpu.VMEM((SLOTS, WIDTH), BF16)],
+        compiler_params=pltpu.CompilerParams(vmem_limit_bytes=60 * 2**20),
+        name="score",
+    )(
+        count,
+        recv.reshape(SLOTS, WIDTH),
+        centre,
+        place,
+        q_all.reshape(PLANE * ITEMS, WIDTH),
+    )
 
 
 def solution(mesh):

time: 81.9 us -> 61.6 us (0.75)
  Pallas kernels: 74 us -> 60.8 us
  local copies, waits for them, and re-layouts: 6.9 us -> 0 us
    pallas_call x1 -> x2, Pallas kernels: 74 us -> 60.8 us  [the longest x1 51 us: per_device(): pl.pallas_call(kernel, out_shape=(jax.ShapeDtypeStruct((PLANE, CAP, WIDTH...]
    unnamed x14 -> x0, local copies, waits for them, and re-layouts: 6.9 us -> none
where the time goes in v2:
time: 61.6 us; the launch traced here: 61.5 us
  Pallas kernels  60.8 us (99%)
  between operations  0.64 us (1%)
    pallas_call x1, Pallas kernels, per_device(): pl.pallas_call(kernel, out_shape=(jax.ShapeDtypeStruct((PLANE, CAP, WIDTH...  51 us
    pallas_call x1, Pallas kernels, per_device(): pl.pallas_call(score_kernel, grid=(PLANE * ITEMS // TILE,), out_shape=(ja...  9.82 us

profile of v2, /device:TPU:1, one launch (start us, length us, event | category | flops | bytes accessed | tf_op | source)
XLA Modules:
  0.0 61.5 jit_solution(848587394908845015)
XLA Ops:
  0.6 51.0 %encode_and_route.1 = (bf16[32,32,256]{2,1,0:T(8,128)(2,1)}, bf16[32,512,256]{2,1,0:T(8,128)(2,1)}, bf16[1024,256]{1,0:T(8,128)(2,1)}, f32[1,1024]{1,0:T(1,128)}, s32[1,128]{1,0:T(1,128)}) custom-call(bf16[512,1024]{1,0:T(8,128)(2,1)} %feat_in.1, bf16[128,1024]{1,0:T(8,128)(2,1)} %wh_in.1, bf16[128,256]{1,0:T(8,128)(2,1)} %wo_in.1, s32[1,512]{1,0:T(1,128)} %bitcast.5, ...), custom_call_target="tpu_custom_call" | custom-call | tf_op jit(solution)/shard_map/encode_and_route/pallas_call | solution.py:395
  51.6 9.8 %score.1 = (bf16[1024,256]{1,0:T(8,128)(2,1)}, f32[1,16384]{1,0:T(1,128)}) custom-call(s32[1,128]{1,0:T(1,128)} %get-tuple-element.7.count_ref, bf16[1024,256]{1,0:T(8,128)(2,1)} %bitcast.4, bf16[1024,256]{1,0:T(8,128)(2,1)} %get-tuple-element.9.centre_ref, f32[1,1024]{1,0:T(1,128)} %get-tuple-element.10.place_ref, bf16[16384,256]{1,0:T(8,128)(2,1)} %bitcast.3), custom_call_target="tpu_custom_call" | custom-call | tf_op jit(solution)/shard_map/score/pallas_call | solution.py:432

commit v3 on v0

v3 whole, which is shorter than its diff:
```python
import jax
import jax.numpy as jnp
from jax import lax
from jax.experimental import pallas as pl
from jax.experimental.pallas import tpu as pltpu
from jax.sharding import PartitionSpec as P

MESH = pl.DeviceIdType.MESH
NY, NX, NC, NZ = 4, 4, 2, 8
PLANE = NY * NX * NC
ITEMS, FEAT, WIDTH, LISTS, CAP = 512, 1024, 256, 128, 32
SLOTS = PLANE * CAP
WCOLS = FEAT + WIDTH
STAGES = ((0, 512), (512, 512), (1024, 256))
ROWS = FEAT // NZ
PART = ITEMS // 2
F32, BF16 = jnp.float32, jnp.bfloat16


def kernel(
    feat_in, wh_in, wo_in, lists_in, cent_in, q_in,
    codes_out, packed_out, q_out, count_out,
    feat, wfull, normed, hid, squares, sel, send, recv, ids_ref, cent, slists, glists, onehot,
    codes, pick, packed, count,
    loc, ws, wz_r, wc_r, qs, q1_r, q2_r, qc_r, ls, lr, av, ar,
):
    me = lax.axis_index("lists")
    z = lax.axis_index("refresh")
    y, x, c = me // (NX * NC), (me // NC) % NX, me % NC

    def at(dy, dx, dc):
        return ((y + dy) % NY * NX + (x + dx) % NX) * NC + (c + dc) % NC

    def to(lists, refresh=None):
        return (z if refresh is None else refresh, lists)

    def push(src, dst, send_sem, recv_sem, device):
        pltpu.make_async_remote_copy(
            src_ref=src, dst_ref=dst, send_sem=send_sem, recv_sem=recv_sem,
            device_id=device, device_id_type=MESH,
        ).start()

    def await_bytes(ref, sem):
        pltpu.make_async_copy(ref, ref, sem).wait()

    def each(low, high, body):
        def step_once(i, _):
            body(i)
            return 0

        lax.fori_loop(low, high, step_once, 0)

    other = to(at(0, 0, 1))

    barrier = pltpu.get_barrier_semaphore()

    def peer_of(k):
        return at(k // 8, (k // 2) % 4, k % 2)

    def greet(device):
        pl.semaphore_signal(barrier, inc=1, device_id=device, device_id_type=MESH)

    each(1, PLANE, lambda k: greet(to(peer_of(k))))
    each(1, NZ, lambda k: greet(to(me, (z + k) % NZ)))
    mine = pl.ds(pl.multiple_of(z * ROWS, ROWS), ROWS)
    q_mine = pl.ds(pl.multiple_of(me * ITEMS, ITEMS), ITEMS)
    own = [
        pltpu.make_async_copy(wh_in, wfull.at[mine, pl.ds(0, FEAT)], loc.at[0]),
        pltpu.make_async_copy(wo_in, wfull.at[mine, pl.ds(FEAT, WIDTH)], loc.at[1]),
        pltpu.make_async_copy(lists_in, ids_ref, loc.at[2]),
        pltpu.make_async_copy(feat_in, feat, loc.at[3]),
        pltpu.make_async_copy(cent_in, cent, loc.at[4]),
        pltpu.make_async_copy(q_in, q_out.at[q_mine], loc.at[5]),
    ]
    for copy in own:
        copy.start()
    for copy in own[:3]:
        copy.wait()
    pl.semaphore_wait(barrier, PLANE - 1 + NZ - 1)

    def shard(stage, plane, core, part=None):
        first, width = STAGES[stage]
        if part is not None:
            width //= 2
            first += part * width
        row = pl.multiple_of(plane * ROWS + core * (ROWS // 2), ROWS // 2)
        return wfull.at[pl.ds(row, ROWS // 2), pl.ds(first, width)]

    def source(hop, way):
        return (z + NZ - hop) % NZ if way == 0 else (z + hop) % NZ

    def pass_z(hop, stage, way):
        part = shard(stage, source(hop - 1, way), c, way if hop == 4 else None)
        there = to(me, (z + 1) % NZ if way == 0 else (z + NZ - 1) % NZ)
        push(part, part, ws.at[0], wz_r.at[hop - 1, stage, way], there)

    def land_z(hop, stage):
        for way in range(2):
            part = shard(stage, source(hop, way), c, way if hop == 4 else None)
            await_bytes(part, wz_r.at[hop - 1, stage, way])
            if hop < 4:
                pass_z(hop + 1, stage, way)
        for way in range(2):
            part = shard(stage, source(hop, way), c, way if hop == 4 else None)
            push(part, part, ws.at[1], wc_r.at[hop - 1, stage, way], other)

    def paired(stage):
        for hop in range(1, 5):
            for way in range(2):
                part = shard(stage, source(hop, way), 1 - c, way if hop == 4 else None)
                await_bytes(part, wc_r.at[hop - 1, stage, way])

    def rows(block, first, size):
        return q_out.at[pl.ds(pl.multiple_of(block * ITEMS + first, 64), size)]

    def half_rows(block, half):
        return rows(block, half * PART, PART)

    def own_rows(half):
        return q_in.at[pl.ds(half * PART, PART)]

    def over(half, d):
        return to(at(d * half, d * (1 - half), 0))

    def block_of(half, e, d):
        return at(4 - d - half * (e - d), 4 - e - half * (d - e), 0)

    def first_leg(half, d):
        push(own_rows(half), half_rows(me, half), qs.at[0], q1_r.at[half, d - 1], over(half, d))

    def second_leg(half, e, d):
        here = half_rows(block_of(half, e, 0), half)
        src = here if e else own_rows(half)
        push(src, here, qs.at[1], q2_r.at[half, e, d - 1], over(1 - half, d))

    def share(half, e, d):
        here = half_rows(block_of(half, e, d), half)
        push(here, here, qs.at[2], qc_r.at[half, e, d], other)

    def land_first(e):
        for half in range(2):
            await_bytes(half_rows(me, half), q1_r.at[half, e - 1])
            share(half, e, 0)
            second_leg(half, e, 1)
            second_leg(half, e, 3)

    def land_second(e, d):
        for half in range(2):
            here = half_rows(block_of(half, e, d), half)
            await_bytes(here, q2_r.at[half, e, d - 1])
            if d == (1 if e < 2 else 3):
                push(here, here, qs.at[1], q2_r.at[half, e, 1], over(1 - half, d))
            share(half, e, d)

    for stage in range(3):
        pass_z(1, stage, 0)
        pass_z(1, stage, 1)
    for d in (1, 3, 2):
        for half in range(2):
            first_leg(half, d)
    for d in (1, 3):
        for half in range(2):
            second_leg(half, 0, d)
    for half in range(2):
        push(own_rows(half), half_rows(me, half), qs.at[2], qc_r.at[half, 0, 0], other)

    ids = ids_ref[...]
    owner = lax.shift_right_logical(ids, 7)
    within = ids - owner * LISTS
    table = (lax.broadcasted_iota(jnp.int32, (PLANE, ITEMS), 0) == owner).astype(F32)
    earlier = (
        lax.broadcasted_iota(jnp.int32, (ITEMS, ITEMS), 0)
        < lax.broadcasted_iota(jnp.int32, (ITEMS, ITEMS), 1)
    ).astype(F32)
    prior = jnp.dot(table.astype(BF16), earlier.astype(BF16), preferred_element_type=F32)
    rank = jnp.sum(prior * table, axis=0, keepdims=True).astype(jnp.int32)
    rank_table = (lax.broadcasted_iota(jnp.int32, (128, ITEMS), 0) == rank).astype(F32)
    marked = table * (within + 1).astype(F32)
    slot_lists = lax.dot_general(
        marked.astype(BF16), rank_table.astype(BF16), (((1,), (1,)), ((), ())),
        preferred_element_type=F32,
    )
    slists[...] = slot_lists.reshape(PLANE, 1, 128)
    each(1, PLANE, lambda k: push(slists.at[peer_of(k)], glists.at[me], ls, lr, to(peer_of(k))))
    glists[me] = slists[me]

    own[3].wait()

    def norm_rows(i):
        r = pl.ds(pl.multiple_of(i * 64, 64), 64)
        v = feat[r, :].astype(F32)
        scale = lax.rsqrt(jnp.mean(v * v, axis=-1, keepdims=True) + 1e-06)
        normed[r, :] = (v * scale).astype(BF16)

    each(0, ITEMS // 64, norm_rows)

    for stage in range(3):
        land_z(1, stage)
    land_first(1)
    land_first(3)
    slot = owner * CAP + rank
    for r in range(0, SLOTS, 256):
        sel[r : r + 256, :] = (
            (lax.broadcasted_iota(jnp.int32, (256, ITEMS), 0) + r == slot).astype(F32).astype(BF16)
        )
    for stage in range(3):
        land_z(2, stage)
    land_first(2)
    for stage in range(3):
        land_z(3, stage)
    land_second(0, 1)
    land_second(0, 3)

    squares[...] = jnp.zeros_like(squares)

    def hidden(j):
        cols = pl.ds(pl.multiple_of(j * 256, 256), 256)
        pre = jnp.dot(normed[...], wfull[:, cols], preferred_element_type=F32)
        gelu = 0.5 * pre * (1.0 + lax.erf(pre * 0.7071067811865476))
        h = (feat[:, cols].astype(F32) + gelu).astype(BF16)
        hid[:, cols] = h
        h = h.astype(F32)
        h = h * h
        squares[...] += h[:, :128] + h[:, 128:]

    land_z(4, 0)
    paired(0)
    each(0, 2, hidden)
    land_z(4, 1)
    land_z(4, 2)
    paired(1)
    each(2, 4, hidden)
    paired(2)
    land_second(1, 1)
    land_second(3, 3)
    total = jnp.sum(squares[...], axis=-1, keepdims=True)
    scale = lax.rsqrt(total * (1.0 / FEAT) + 1e-06)
    out = jnp.dot(hid[...], wfull[:, FEAT:], preferred_element_type=F32)
    normed[:, :WIDTH] = (out * scale).astype(BF16)
    for i in range(4):
        out = jnp.dot(
            sel[i * 256 : (i + 1) * 256, :], normed[:, :WIDTH], preferred_element_type=F32
        )
        send[i * 8 : (i + 1) * 8] = out.astype(BF16).reshape(8, CAP, WIDTH)

    each(1, PLANE, lambda k: push(send.at[peer_of(k)], recv.at[me], av, ar, to(peer_of(k))))
    recv[me] = send[me]
    for e, d in ((2, 3), (1, 3), (3, 1), (2, 1)):
        land_second(e, d)

    own[4].wait()
    await_bytes(glists.at[pl.ds(0, PLANE - 1)], lr)
    marks = jnp.transpose(glists[...].reshape(PLANE, 128))
    lane = lax.broadcasted_iota(jnp.int32, (CAP, LISTS), 1).astype(F32) + 1.0
    for s in range(PLANE):
        column = marks[:CAP, s : s + 1]
        onehot[s * CAP : (s + 1) * CAP, :] = (column == lane).astype(F32).astype(BF16)
    centre = jnp.dot(onehot[...], cent[...], preferred_element_type=F32)
    held = jnp.sum((marks > 0.5).astype(F32), axis=0, keepdims=True)
    below = (
        lax.broadcasted_iota(jnp.int32, (PLANE, PLANE), 0)
        < lax.broadcasted_iota(jnp.int32, (PLANE, PLANE), 1)
    ).astype(F32)
    start = jnp.dot(held.astype(BF16), below.astype(BF16), preferred_element_type=F32)
    high = jnp.floor(start * (1.0 / CAP))
    low = start - high * CAP
    source = lax.shift_right_logical(lax.broadcasted_iota(jnp.int32, (PLANE, SLOTS), 1), 5)
    member = (lax.broadcasted_iota(jnp.int32, (PLANE, SLOTS), 0) == source).astype(F32).astype(BF16)

    def spread_out(row):
        return jnp.dot(row.astype(BF16), member, preferred_element_type=F32)

    within_source = (lax.broadcasted_iota(jnp.int32, (1, SLOTS), 1) & (CAP - 1)).astype(F32)
    place = jnp.where(
        within_source < spread_out(held),
        spread_out(high) * CAP + spread_out(low) + within_source,
        -1.0,
    )
    filled = jnp.sum(held, axis=1, keepdims=True)
    count[...] = jnp.broadcast_to(filled, (1, 128)).astype(jnp.int32)
    last = jnp.maximum(filled - 1.0, 0.0)
    for r in range(0, SLOTS, 256):
        row = (lax.broadcasted_iota(jnp.int32, (256, SLOTS), 0) + r).astype(F32)
        pick[r : r + 256, :] = (jnp.minimum(row, last) == place).astype(F32).astype(BF16)

    for e in (0, 1, 3, 2):
        land_second(e, 2)
    own[5].wait()
    await_bytes(recv.at[pl.ds(0, PLANE - 1)], ar)
    codes[...] = (recv[...].reshape(SLOTS, WIDTH).astype(F32) - centre).astype(BF16)
    results = [
        pltpu.make_async_copy(codes, codes_out, loc.at[6]),
        pltpu.make_async_copy(packed, packed_out, loc.at[7]),
        pltpu.make_async_copy(count, count_out, loc.at[8]),
    ]
    results[0].start()
    results[2].start()
    for r in range(0, SLOTS, 256):
        packed[r : r + 256, :] = jnp.dot(
            pick[r : r + 256, :], codes[...], preferred_element_type=F32
        ).astype(BF16)
    results[1].start()

    def shared(k):
        for half in range(2):
            await_bytes(half_rows(me, half), qc_r.at[half, k // 4, k % 4])

    each(0, 16, shared)

    await_bytes(wfull.at[pl.ds(0, 7 * 64)], ws.at[0])
    await_bytes(wfull.at[pl.ds(0, 7 * 64)], ws.at[1])
    await_bytes(q_out.at[pl.ds(0, 6 * PART)], qs.at[0])
    await_bytes(q_out.at[pl.ds(0, 24 * PART)], qs.at[1])
    await_bytes(q_out.at[pl.ds(0, 16 * ITEMS)], qs.at[2])
    await_bytes(slists.at[pl.ds(0, PLANE - 1)], ls)
    await_bytes(send.at[pl.ds(0, PLANE - 1)], av)
    for copy in results:
        copy.wait()


VARIANTS = (256, 512, 576, 640, 704, 768, 1024)
TILE = 4096


def score_kernel(count_ref, codes_ref, packed_ref, q_ref, out_ref, best_ref):
    count = count_ref[0, 0]

    @pl.when(pl.program_id(0) == 0)
    def _():
        out_ref[...] = codes_ref[...]

    for at, size in enumerate(VARIANTS):
        less = VARIANTS[at - 1] if at else 0

        @pl.when((count > less) & (count <= size))
        def _():
            for lo in range(0, TILE, 256):
                s = lax.dot_general(
                    packed_ref[:size, :], q_ref[lo : lo + 256, :], (((1,), (1,)), ((), ())),
                    preferred_element_type=F32,
                )
                best_ref[:, lo : lo + 256] = jnp.max(s, axis=0, keepdims=True)

    @pl.when(count == 0)
    def _():
        best_ref[...] = jnp.full_like(best_ref, -1e30)


def per_device(features, w_hidden, w_out, list_ids, centroids, queries):
    anywhere = pl.BlockSpec(memory_space=pl.ANY)
    dma = pltpu.SemaphoreType.DMA
    codes, packed, q_all, count = pl.pallas_call(
        kernel,
        out_shape=(
            jax.ShapeDtypeStruct((SLOTS, WIDTH), BF16),
            jax.ShapeDtypeStruct((SLOTS, WIDTH), BF16),
            jax.ShapeDtypeStruct((PLANE * ITEMS, WIDTH), BF16),
            jax.ShapeDtypeStruct((1, 128), jnp.int32),
        ),
        in_specs=[anywhere] * 6,
        out_specs=(anywhere,) * 4,
        scratch_shapes=[
            pltpu.VMEM((ITEMS, FEAT), BF16),
            pltpu.VMEM((FEAT, WCOLS), BF16),
            pltpu.VMEM((ITEMS, FEAT), BF16),
            pltpu.VMEM((ITEMS, FEAT), BF16),
            pltpu.VMEM((ITEMS, 128), F32),
            pltpu.VMEM((SLOTS, ITEMS), BF16),
            pltpu.VMEM((PLANE, CAP, WIDTH), BF16),
            pltpu.VMEM((PLANE, CAP, WIDTH), BF16),
            pltpu.VMEM((1, ITEMS), jnp.int32),
            pltpu.VMEM((LISTS, WIDTH), BF16),
            pltpu.VMEM((PLANE, 1, 128), F32),
            pltpu.VMEM((PLANE, 1, 128), F32),
            pltpu.VMEM((SLOTS, LISTS), BF16),
            pltpu.VMEM((SLOTS, WIDTH), BF16),
            pltpu.VMEM((SLOTS, SLOTS), BF16),
            pltpu.VMEM((SLOTS, WIDTH), BF16),
            pltpu.VMEM((1, 128), jnp.int32),
            dma((9,)), dma((2,)), dma((4, 3, 2)), dma((4, 3, 2)),
            dma((3,)), dma((2, 3)), dma((2, 4, 3)), dma((2, 4, 4)),
            dma, dma, dma, dma,
        ],
        compiler_params=pltpu.CompilerParams(
            collective_id=0, has_side_effects=True, vmem_limit_bytes=62 * 2**20
        ),
        name="encode_and_route",
    )(features, w_hidden, w_out, list_ids.reshape(1, ITEMS), centroids, queries)
    whole = pl.BlockSpec((SLOTS, WIDTH), lambda i: (0, 0))
    return pl.pallas_call(
        score_kernel,
        grid=(PLANE * ITEMS // TILE,),
        out_shape=(
            jax.ShapeDtypeStruct((SLOTS, WIDTH), BF16),
            jax.ShapeDtypeStruct((1, PLANE * ITEMS), F32),
        ),
        in_specs=[
            pl.BlockSpec(memory_space=pltpu.SMEM),
            whole,
            whole,
            pl.BlockSpec((TILE, WIDTH), lambda i: (i, 0)),
        ],
        out_specs=(whole, pl.BlockSpec((1, TILE), lambda i: (0, i))),
        compiler_params=pltpu.CompilerParams(vmem_limit_bytes=60 * 2**20),
        name="score",
    )(count, codes, packed, q_all)


def solution(mesh):
    in_specs = (
        P(("refresh", "lists"), None),
        P("refresh", None),
        P("refresh", None),
        P(("refresh", "lists")),
        P("lists", None),
        P("lists", None),
    )
    out_specs = (P(("refresh", "lists"), None), P(("refresh", "lists"), None))
    return jax.shard_map(
        per_device, mesh=mesh, in_specs=in_specs, out_specs=out_specs, check_vma=False
    )
```

time: 140 us -> 56 us (0.40)
  Pallas kernels: 0 us -> 55.2 us
  waiting for transfers between devices: 49.2 us -> 0 us
  blocking collectives: 26.6 us -> 0 us
  matrix products: 22.2 us -> 0 us
  starting transfers between devices: 18.3 us -> 0 us
  between operations: 14.1 us -> 0.64 us
  local copies, waits for them, and re-layouts: 6.46 us -> 0 us
  other arithmetic: 2.33 us -> 0 us
    pallas_call x0 -> x2, Pallas kernels: none -> 55.2 us  [the longest x1 46.6 us: per_device(): pl.pallas_call(kernel, out_shape=(jax.ShapeDtypeStruct((SLOTS, WIDTH), BF...]
    all_gather x2 -> x0, waiting for transfers between devices: 35.5 us -> none  [the longest x1 30.8 us: per_device(): lax.all_gather(queries, 'lists', axis=0, tiled=True)]
    all_gather x1 -> x0, blocking collectives: 26.6 us -> none  [per_device(): lax.all_gather(w_out, 'refresh', axis=0, tiled=True)]
    dot_general x5 -> x0, matrix products: 22.2 us -> none  [the longest x1 13.5 us: best_for(): jnp.dot(query_block, block_codes.T, preferred_element_type=jnp.float32)]
    all_to_all x2 -> x0, starting transfers between devices: 18.2 us -> none  [the longest x1 9.66 us: per_device(): lax.all_to_all(send_rows, 'lists', split_axis=0, concat_axis=0, tiled=True)]
    all_to_all x2 -> x0, waiting for transfers between devices: 12.4 us -> none  [the longest x1 12.4 us: per_device(): lax.all_to_all(send_rows, 'lists', split_axis=0, concat_axis=0, tiled=True)]
    scatter x2 -> x0, local copies, waits for them, and re-layouts: 5.58 us -> none  [the longest x1 3.14 us: per_device(): jnp.zeros((owners_count * capacity, width_out), jnp.bfloat16).at[slots]]
    reduce_sum x1 -> x0, other arithmetic: 1.5 us -> none  [root_scale(): jnp.mean(values * values, axis=-1, keepdims=True) + 1e-06]
  transfers between devices with their start and end apart: 4 -> 0, of which waited for: 3 -> 0; matrix products, arithmetic and copies ran while one was open for 12% -> 0% of each run, Pallas kernels for 0% -> 0%
where the time goes in v3:
time: 56 us; the launch traced here: 55.8 us
  Pallas kernels  55.2 us (99%)
  between operations  0.64 us (1%)
    pallas_call x1, Pallas kernels, per_device(): pl.pallas_call(kernel, out_shape=(jax.ShapeDtypeStruct((SLOTS, WIDTH), BF...  46.6 us
    pallas_call x1, Pallas kernels, per_device(): pl.pallas_call(score_kernel, grid=(PLANE * ITEMS // TILE,), out_shape=(ja...  8.61 us

profile of v3, /device:TPU:1, one launch (start us, length us, event | category | flops | bytes accessed | tf_op | source)
XLA Modules:
  0.0 55.8 jit_solution(2974531017034719363)
XLA Ops:
  0.6 46.6 %encode_and_route.1 = (bf16[1024,256]{1,0:T(8,128)(2,1)}, bf16[1024,256]{1,0:T(8,128)(2,1)}, bf16[16384,256]{1,0:T(8,128)(2,1)}, s32[1,128]{1,0:T(1,128)}) custom-call(bf16[512,1024]{1,0:T(8,128)(2,1)} %feat_in.1, bf16[128,1024]{1,0:T(8,128)(2,1)} %wh_in.1, bf16[128,256]{1,0:T(8,128)(2,1)} %wo_in.1, s32[1,512]{1,0:T(1,128)} %bitcast.1, ...), custom_call_target="tpu_custom_call" | custom-call | tf_op jit(solution)/shard_map/encode_and_route/pallas_call | solution.py:352
  47.2 8.6 %score.1 = (bf16[1024,256]{1,0:T(8,128)(2,1)}, f32[1,16384]{1,0:T(1,128)}) custom-call(s32[1,128]{1,0:T(1,128)} %get-tuple-element.6.count_ref, bf16[1024,256]{1,0:T(8,128)(2,1)} %get-tuple-element.7.codes_ref, bf16[1024,256]{1,0:T(8,128)(2,1)} %get-tuple-element.8.packed_ref, bf16[16384,256]{1,0:T(8,128)(2,1)} %get-tuple-element.9.q_ref), custom_call_target="tpu_custom_call" | custom-call | tf_op jit(solution)/shard_map/score/pallas_call | solution.py:390

commit v4 on v3

--- a/solution.py
+++ b/solution.py
@@ -20,7 +20,7 @@
 def kernel(
     feat_in, wh_in, wo_in, lists_in, cent_in, q_in,
     codes_out, packed_out, q_out, count_out,
-    feat, wfull, normed, hid, squares, sel, send, recv, ids_ref, cent, slists, glists, onehot,
+    q_own, feat, wfull, normed, hid, squares, sel, send, recv, ids_ref, cent, slists, glists,
     codes, pick, packed, count,
     loc, ws, wz_r, wc_r, qs, q1_r, q2_r, qc_r, ls, lr, av, ar,
 ):
@@ -61,7 +61,8 @@
         pl.semaphore_signal(barrier, inc=1, device_id=device, device_id_type=MESH)
 
     each(1, PLANE, lambda k: greet(to(peer_of(k))))
-    each(1, NZ, lambda k: greet(to(me, (z + k) % NZ)))
+    greet(to(me, (z + 1) % NZ))
+    greet(to(me, (z + NZ - 1) % NZ))
     mine = pl.ds(pl.multiple_of(z * ROWS, ROWS), ROWS)
     q_mine = pl.ds(pl.multiple_of(me * ITEMS, ITEMS), ITEMS)
     own = [
@@ -70,13 +71,14 @@
         pltpu.make_async_copy(lists_in, ids_ref, loc.at[2]),
         pltpu.make_async_copy(feat_in, feat, loc.at[3]),
         pltpu.make_async_copy(cent_in, cent, loc.at[4]),
-        pltpu.make_async_copy(q_in, q_out.at[q_mine], loc.at[5]),
+        pltpu.make_async_copy(q_in, q_own, loc.at[5]),
     ]
     for copy in own:
         copy.start()
-    for copy in own[:3]:
-        copy.wait()
-    pl.semaphore_wait(barrier, PLANE - 1 + NZ - 1)
+    own[5].wait()
+    keep_q = pltpu.make_async_copy(q_own, q_out.at[q_mine], loc.at[9])
+    keep_q.start()
+    pl.semaphore_wait(barrier, PLANE - 1 + 2)
 
     def shard(stage, plane, core, part=None):
         first, width = STAGES[stage]
@@ -92,7 +94,15 @@
     def pass_z(hop, stage, way):
         part = shard(stage, source(hop - 1, way), c, way if hop == 4 else None)
         there = to(me, (z + 1) % NZ if way == 0 else (z + NZ - 1) % NZ)
-        push(part, part, ws.at[0], wz_r.at[hop - 1, stage, way], there)
+        src = part
+        if hop == 1:
+            first, width = STAGES[stage]
+            held = wo_in if first == FEAT else wh_in
+            src = held.at[
+                pl.ds(pl.multiple_of(c * (ROWS // 2), ROWS // 2), ROWS // 2),
+                pl.ds(first % FEAT, width),
+            ]
+        push(src, part, ws.at[0], wz_r.at[hop - 1, stage, way], there)
 
     def land_z(hop, stage):
         for way in range(2):
@@ -117,7 +127,7 @@
         return rows(block, half * PART, PART)
 
     def own_rows(half):
-        return q_in.at[pl.ds(half * PART, PART)]
+        return q_own.at[pl.ds(half * PART, PART)]
 
     def over(half, d):
         return to(at(d * half, d * (1 - half), 0))
@@ -164,6 +174,7 @@
     for half in range(2):
         push(own_rows(half), half_rows(me, half), qs.at[2], qc_r.at[half, 0, 0], other)
 
+    own[2].wait()
     ids = ids_ref[...]
     owner = lax.shift_right_logical(ids, 7)
     within = ids - owner * LISTS
@@ -184,32 +195,34 @@
     each(1, PLANE, lambda k: push(slists.at[peer_of(k)], glists.at[me], ls, lr, to(peer_of(k))))
     glists[me] = slists[me]
 
-    own[3].wait()
-
-    def norm_rows(i):
-        r = pl.ds(pl.multiple_of(i * 64, 64), 64)
-        v = feat[r, :].astype(F32)
-        scale = lax.rsqrt(jnp.mean(v * v, axis=-1, keepdims=True) + 1e-06)
-        normed[r, :] = (v * scale).astype(BF16)
-
-    each(0, ITEMS // 64, norm_rows)
-
     for stage in range(3):
         land_z(1, stage)
     land_first(1)
     land_first(3)
-    slot = owner * CAP + rank
-    for r in range(0, SLOTS, 256):
-        sel[r : r + 256, :] = (
-            (lax.broadcasted_iota(jnp.int32, (256, ITEMS), 0) + r == slot).astype(F32).astype(BF16)
-        )
+    own[3].wait()
+
+    def norm_rows(i):
+        r = pl.ds(pl.multiple_of(i * 128, 128), 128)
+        v = feat[r, :].astype(F32)
+        scale = lax.rsqrt(jnp.mean(v * v, axis=-1, keepdims=True) + 1e-06)
+        normed[r, :] = (v * scale).astype(BF16)
+
+    each(0, ITEMS // 128, norm_rows)
+    land_first(2)
     for stage in range(3):
         land_z(2, stage)
-    land_first(2)
+    land_second(0, 1)
+    land_second(0, 3)
+    slot = owner * CAP + rank
+
+    def select(i):
+        r = pl.multiple_of(i * 128, 128)
+        row = lax.broadcasted_iota(jnp.int32, (128, ITEMS), 0) + r
+        sel[pl.ds(r, 128), :] = (row == slot).astype(F32).astype(BF16)
+
+    each(0, SLOTS // 128, select)
     for stage in range(3):
         land_z(3, stage)
-    land_second(0, 1)
-    land_second(0, 3)
 
     squares[...] = jnp.zeros_like(squares)
 
@@ -224,6 +237,8 @@
         squares[...] += h[:, :128] + h[:, 128:]
 
     land_z(4, 0)
+    own[0].wait()
+    own[1].wait()
     paired(0)
     each(0, 2, hidden)
     land_z(4, 1)
@@ -237,13 +252,22 @@
     scale = lax.rsqrt(total * (1.0 / FEAT) + 1e-06)
     out = jnp.dot(hid[...], wfull[:, FEAT:], preferred_element_type=F32)
     normed[:, :WIDTH] = (out * scale).astype(BF16)
-    for i in range(4):
-        out = jnp.dot(
-            sel[i * 256 : (i + 1) * 256, :], normed[:, :WIDTH], preferred_element_type=F32
-        )
-        send[i * 8 : (i + 1) * 8] = out.astype(BF16).reshape(8, CAP, WIDTH)
-
-    each(1, PLANE, lambda k: push(send.at[peer_of(k)], recv.at[me], av, ar, to(peer_of(k))))
+
+    def route(i):
+        dy = (i * 3 + 2) % 4
+        there = (y + dy) % NY
+        r = pl.multiple_of(there * 256, 256)
+        out = jnp.dot(sel[pl.ds(r, 256), :], normed[:, :WIDTH], preferred_element_type=F32)
+        send[pl.ds(there * 8, 8)] = out.astype(BF16).reshape(8, CAP, WIDTH)
+        for dx in (2, 1, 3, 0):
+            for dc in (1, 0):
+                peer = at(dy, dx, dc)
+
+                @pl.when(peer != me)
+                def _():
+                    push(send.at[peer], recv.at[me], av, ar, to(peer))
+
+    each(0, 4, route)
     recv[me] = send[me]
     for e, d in ((2, 3), (1, 3), (3, 1), (2, 1)):
         land_second(e, d)
@@ -251,11 +275,6 @@
     own[4].wait()
     await_bytes(glists.at[pl.ds(0, PLANE - 1)], lr)
     marks = jnp.transpose(glists[...].reshape(PLANE, 128))
-    lane = lax.broadcasted_iota(jnp.int32, (CAP, LISTS), 1).astype(F32) + 1.0
-    for s in range(PLANE):
-        column = marks[:CAP, s : s + 1]
-        onehot[s * CAP : (s + 1) * CAP, :] = (column == lane).astype(F32).astype(BF16)
-    centre = jnp.dot(onehot[...], cent[...], preferred_element_type=F32)
     held = jnp.sum((marks > 0.5).astype(F32), axis=0, keepdims=True)
     below = (
         lax.broadcasted_iota(jnp.int32, (PLANE, PLANE), 0)
@@ -276,16 +295,27 @@
         spread_out(high) * CAP + spread_out(low) + within_source,
         -1.0,
     )
+    every = jnp.dot(marks[:CAP, :].astype(BF16), member, preferred_element_type=F32)
+    ranks = lax.broadcasted_iota(jnp.int32, (CAP, SLOTS), 0).astype(F32)
+    list_row = jnp.sum(jnp.where(ranks == within_source, every, 0.0), axis=0, keepdims=True)
+    lists = lax.broadcasted_iota(jnp.int32, (LISTS, SLOTS), 0).astype(F32) + 1.0
+    centre = lax.dot_general(
+        (lists == list_row).astype(F32).astype(BF16), cent[...], (((0,), (0,)), ((), ())),
+        preferred_element_type=F32,
+    )
     filled = jnp.sum(held, axis=1, keepdims=True)
     count[...] = jnp.broadcast_to(filled, (1, 128)).astype(jnp.int32)
     last = jnp.maximum(filled - 1.0, 0.0)
-    for r in range(0, SLOTS, 256):
-        row = (lax.broadcasted_iota(jnp.int32, (256, SLOTS), 0) + r).astype(F32)
-        pick[r : r + 256, :] = (jnp.minimum(row, last) == place).astype(F32).astype(BF16)
-
+
+    def choose(i):
+        r = pl.multiple_of(i * 128, 128)
+        row = (lax.broadcasted_iota(jnp.int32, (128, SLOTS), 0) + r).astype(F32)
+        pick[pl.ds(r, 128), :] = (jnp.minimum(row, last) == place).astype(F32).astype(BF16)
+
+    each(0, SLOTS // 128, choose)
     for e in (0, 1, 3, 2):
         land_second(e, 2)
-    own[5].wait()
+    keep_q.wait()
     await_bytes(recv.at[pl.ds(0, PLANE - 1)], ar)
     codes[...] = (recv[...].reshape(SLOTS, WIDTH).astype(F32) - centre).astype(BF16)
     results = [
@@ -295,10 +325,12 @@
     ]
     results[0].start()
     results[2].start()
-    for r in range(0, SLOTS, 256):
-        packed[r : r + 256, :] = jnp.dot(
-            pick[r : r + 256, :], codes[...], preferred_element_type=F32
-        ).astype(BF16)
+
+    def pack(i):
+        r = pl.ds(pl.multiple_of(i * 256, 256), 256)
+        packed[r, :] = jnp.dot(pick[r, :], codes[...], preferred_element_type=F32).astype(BF16)
+
+    each(0, 4, pack)
     results[1].start()
 
     def shared(k):
@@ -318,16 +350,14 @@
         copy.wait()
 
 
-VARIANTS = (256, 512, 576, 640, 704, 768, 1024)
+VARIANTS = (256, 512, 544, 576, 608, 640, 704, 768, 1024)
 TILE = 4096
 
 
 def score_kernel(count_ref, codes_ref, packed_ref, q_ref, out_ref, best_ref):
     count = count_ref[0, 0]
 
-    @pl.when(pl.program_id(0) == 0)
-    def _():
-        out_ref[...] = codes_ref[...]
+    out_ref[...] = codes_ref[...]
 
     for at, size in enumerate(VARIANTS):
         less = VARIANTS[at - 1] if at else 0
@@ -360,6 +390,7 @@
         in_specs=[anywhere] * 6,
         out_specs=(anywhere,) * 4,
         scratch_shapes=[
+            pltpu.VMEM((ITEMS, WIDTH), BF16),
             pltpu.VMEM((ITEMS, FEAT), BF16),
             pltpu.VMEM((FEAT, WCOLS), BF16),
             pltpu.VMEM((ITEMS, FEAT), BF16),
@@ -372,12 +403,11 @@
             pltpu.VMEM((LISTS, WIDTH), BF16),
             pltpu.VMEM((PLANE, 1, 128), F32),
             pltpu.VMEM((PLANE, 1, 128), F32),
-            pltpu.VMEM((SLOTS, LISTS), BF16),
             pltpu.VMEM((SLOTS, WIDTH), BF16),
             pltpu.VMEM((SLOTS, SLOTS), BF16),
             pltpu.VMEM((SLOTS, WIDTH), BF16),
             pltpu.VMEM((1, 128), jnp.int32),
-            dma((9,)), dma((2,)), dma((4, 3, 2)), dma((4, 3, 2)),
+            dma((10,)), dma((2,)), dma((4, 3, 2)), dma((4, 3, 2)),
             dma((3,)), dma((2, 3)), dma((2, 4, 3)), dma((2, 4, 4)),
             dma, dma, dma, dma,
         ],
@@ -386,21 +416,22 @@
         ),
         name="encode_and_route",
     )(features, w_hidden, w_out, list_ids.reshape(1, ITEMS), centroids, queries)
-    whole = pl.BlockSpec((SLOTS, WIDTH), lambda i: (0, 0))
+    steps = PLANE * ITEMS // TILE
+    part = pl.BlockSpec((SLOTS // steps, WIDTH), lambda i: (i, 0))
     return pl.pallas_call(
         score_kernel,
-        grid=(PLANE * ITEMS // TILE,),
+        grid=(steps,),
         out_shape=(
             jax.ShapeDtypeStruct((SLOTS, WIDTH), BF16),
             jax.ShapeDtypeStruct((1, PLANE * ITEMS), F32),
         ),
         in_specs=[
             pl.BlockSpec(memory_space=pltpu.SMEM),
-            whole,
-            whole,
+            part,
+            pl.BlockSpec((SLOTS, WIDTH), lambda i: (0, 0)),
             pl.BlockSpec((TILE, WIDTH), lambda i: (i, 0)),
         ],
-        out_specs=(whole, pl.BlockSpec((1, TILE), lambda i: (0, i))),
+        out_specs=(part, pl.BlockSpec((1, TILE), lambda i: (0, i))),
         compiler_params=pltpu.CompilerParams(vmem_limit_bytes=60 * 2**20),
         name="score",
     )(count, codes, packed, q_all)

time: 56 us -> 56 us (level)
  no operation moved by 1% of the time
where the time goes in v4:
time: 56 us; the launch traced here: 55.8 us
  Pallas kernels  55.2 us (99%)
  between operations  0.64 us (1%)
    pallas_call x1, Pallas kernels, per_device(): pl.pallas_call(kernel, out_shape=(jax.ShapeDtypeStruct((SLOTS, WIDTH), BF...  46.7 us
    pallas_call x1, Pallas kernels, per_device(): pl.pallas_call(score_kernel, grid=(steps,), out_shape=(jax.ShapeDtypeStru...  8.54 us

profile of v4, /device:TPU:1, one launch (start us, length us, event | category | flops | bytes accessed | tf_op | source)
XLA Modules:
  0.0 55.8 jit_solution(6008667351455093875)
XLA Ops:
  0.6 46.7 %encode_and_route.1 = (bf16[1024,256]{1,0:T(8,128)(2,1)}, bf16[1024,256]{1,0:T(8,128)(2,1)}, bf16[16384,256]{1,0:T(8,128)(2,1)}, s32[1,128]{1,0:T(1,128)}) custom-call(bf16[512,1024]{1,0:T(8,128)(2,1)} %feat_in.1, bf16[128,1024]{1,0:T(8,128)(2,1)} %wh_in.1, bf16[128,256]{1,0:T(8,128)(2,1)} %wo_in.1, s32[1,512]{1,0:T(1,128)} %bitcast.1, ...), custom_call_target="tpu_custom_call" | custom-call | tf_op jit(solution)/shard_map/encode_and_route/pallas_call | solution.py:382
  47.3 8.5 %score.1 = (bf16[1024,256]{1,0:T(8,128)(2,1)}, f32[1,16384]{1,0:T(1,128)}) custom-call(s32[1,128]{1,0:T(1,128)} %get-tuple-element.6.count_ref, bf16[1024,256]{1,0:T(8,128)(2,1)} %get-tuple-element.7.codes_ref, bf16[1024,256]{1,0:T(8,128)(2,1)} %get-tuple-element.8.packed_ref, bf16[16384,256]{1,0:T(8,128)(2,1)} %get-tuple-element.9.q_ref), custom_call_target="tpu_custom_call" | custom-call | tf_op jit(solution)/shard_map/score/pallas_call | solution.py:421

commit v5 on v4

--- a/solution.py
+++ b/solution.py
@@ -329,9 +329,9 @@
     def pack(i):
         r = pl.ds(pl.multiple_of(i * 256, 256), 256)
         packed[r, :] = jnp.dot(pick[r, :], codes[...], preferred_element_type=F32).astype(BF16)
+        pltpu.make_async_copy(packed.at[r], packed_out.at[r], loc.at[7]).start()
 
     each(0, 4, pack)
-    results[1].start()
 
     def shared(k):
         for half in range(2):

time: 56 us -> 56.1 us (level)
  no operation moved by 1% of the time
where the time goes in v5:
time: 56.1 us; the launch traced here: 55.8 us
  Pallas kernels  55.2 us (98%)
  between operations  0.64 us (1%)
    pallas_call x1, Pallas kernels, per_device(): pl.pallas_call(kernel, out_shape=(jax.ShapeDtypeStruct((SLOTS, WIDTH), BF...  46.7 us
    pallas_call x1, Pallas kernels, per_device(): pl.pallas_call(score_kernel, grid=(steps,), out_shape=(jax.ShapeDtypeStru...  8.54 us

profile of v5, /device:TPU:1, one launch (start us, length us, event | category | flops | bytes accessed | tf_op | source)
XLA Modules:
  0.0 55.8 jit_solution(2252400447043452505)
XLA Ops:
  0.6 46.7 %encode_and_route.1 = (bf16[1024,256]{1,0:T(8,128)(2,1)}, bf16[1024,256]{1,0:T(8,128)(2,1)}, bf16[16384,256]{1,0:T(8,128)(2,1)}, s32[1,128]{1,0:T(1,128)}) custom-call(bf16[512,1024]{1,0:T(8,128)(2,1)} %feat_in.1, bf16[128,1024]{1,0:T(8,128)(2,1)} %wh_in.1, bf16[128,256]{1,0:T(8,128)(2,1)} %wo_in.1, s32[1,512]{1,0:T(1,128)} %bitcast.1, ...), custom_call_target="tpu_custom_call" | custom-call | tf_op jit(solution)/shard_map/encode_and_route/pallas_call | solution.py:382
  47.3 8.5 %score.1 = (bf16[1024,256]{1,0:T(8,128)(2,1)}, f32[1,16384]{1,0:T(1,128)}) custom-call(s32[1,128]{1,0:T(1,128)} %get-tuple-element.6.count_ref, bf16[1024,256]{1,0:T(8,128)(2,1)} %get-tuple-element.7.codes_ref, bf16[1024,256]{1,0:T(8,128)(2,1)} %get-tuple-element.8.packed_ref, bf16[16384,256]{1,0:T(8,128)(2,1)} %get-tuple-element.9.q_ref), custom_call_target="tpu_custom_call" | custom-call | tf_op jit(solution)/shard_map/score/pallas_call | solution.py:421
